TPU v7x, 128 devices: a whole 4x4x4 slice. The times are simulated.
128 devices in a mesh: row: 8 (over x, core), col: 16 (over y, z).
Axes of the slice: x: 4, y: 4, z: 4, core: 2. Of those that a mesh axis runs over, the one named last changes fastest.
Arguments:
- object_field: float32 [2, 4096, 8192], P(None, 'row', 'col'), may hold values from -5 to 5
- probe_field: float32 [2, 256, 256], replicated, may hold values from -6 to 6
- measured: float32 [2048, 256, 256], P(('row', 'col')), may hold values from 0 to 2
- positions: int32 [2048, 2], P(('row', 'col')), may hold values from 0 to 7936, as said below
- counts: int32 [128], replicated, may hold values from 1 to 16, as said below
Outputs:
- new_object: float32 [2, 4096, 8192], P(None, 'row', 'col')
- new_probe: float32 [2, 256, 256], replicated
Inputs may be any that keep to these rules, and one draw needn't show every extreme that they name: `positions`: each slot's window lies whole in the object, and its top-left cell lies in the tile of the device that holds the slot (tiles of 512 x 512 cells in row-major device order). `counts`: some device's bucket is full.
All inputs are finite; a program needn't handle non-finite values.
Results may differ from a plain program's by a relative error of at most 0.0003.
Values sent between devices are 32-bit elements; how exact they have to be, the bound alone decides.
No kernel may reach another device: no remote copies, remote signals or barrier semaphores. Data moves between devices by JAX's collectives and lax.ppermute only.
A program may use at most 128 MiB of HBM per device.

v0:
```python
import math

import jax
import jax.numpy as jnp
from jax import lax
from jax.sharding import PartitionSpec as P

AMPLITUDE_FLOOR = 0.25
OBJECT_RATE = 0.5


def passed_along(shard, axis, by):
    peers = lax.axis_size(axis)
    pairs = [(i, i + by) for i in range(peers) if 0 <= i + by < peers]
    return lax.ppermute(shard, axis, pairs)


def dft_tables(patch_size):
    row_iota = lax.broadcasted_iota(jnp.int32, (patch_size, patch_size), 0)
    col_iota = lax.broadcasted_iota(jnp.int32, (patch_size, patch_size), 1)
    phase_angle = (row_iota * col_iota % patch_size).astype(jnp.float32) * (
        2.0 * math.pi / patch_size
    )
    norm_scale = 1.0 / math.sqrt(patch_size)
    return (jnp.cos(phase_angle) * norm_scale, jnp.sin(phase_angle) * norm_scale)


def matmul(left_side, right_side):
    return jnp.dot(
        left_side, right_side, precision=lax.Precision.HIGHEST, preferred_element_type=jnp.float32
    )


def exit_update(object_patch, probe_field, amplitude, cosine_table, sine_table):
    probe_re, probe_im = (probe_field[0], probe_field[1])
    patch_re, patch_im = (object_patch[0], object_patch[1])
    exit_re = probe_re * patch_re - probe_im * patch_im
    exit_im = probe_re * patch_im + probe_im * patch_re
    left_re = matmul(cosine_table, exit_re) + matmul(sine_table, exit_im)
    left_im = matmul(cosine_table, exit_im) - matmul(sine_table, exit_re)
    spec_re = matmul(left_re, cosine_table) + matmul(left_im, sine_table)
    spec_im = matmul(left_im, cosine_table) - matmul(left_re, sine_table)
    magnitude = jnp.sqrt(spec_re * spec_re + spec_im * spec_im)
    factor = amplitude / jnp.maximum(magnitude, AMPLITUDE_FLOOR)
    proj_re = spec_re * factor
    proj_im = spec_im * factor
    inner_re = matmul(cosine_table, proj_re) - matmul(sine_table, proj_im)
    inner_im = matmul(cosine_table, proj_im) + matmul(sine_table, proj_re)
    back_re = matmul(inner_re, cosine_table) - matmul(inner_im, sine_table)
    back_im = matmul(inner_im, cosine_table) + matmul(inner_re, sine_table)
    diff_re = back_re - exit_re
    diff_im = back_im - exit_im
    object_term = jnp.stack(
        [probe_re * diff_re + probe_im * diff_im, probe_re * diff_im - probe_im * diff_re]
    )
    probe_term = jnp.stack(
        [patch_re * diff_re + patch_im * diff_im, patch_re * diff_im - patch_im * diff_re]
    )
    return (object_term, probe_term)


def per_device(object_field, probe_field, measured, positions, counts):
    tile_rows = object_field.shape[1]
    tile_cols = object_field.shape[2]
    patch_size = probe_field.shape[1]
    zero_index = jnp.int32(0)
    row_pos = lax.axis_index("row")
    col_pos = lax.axis_index("col")
    col_count = lax.axis_size("col")
    own_device = row_pos * col_count + col_pos
    lower_rim = passed_along(object_field[:, :patch_size, :], "row", -1)
    extended_rows = jnp.concatenate([object_field, lower_rim], axis=1)
    right_rim = passed_along(extended_rows[:, :, :patch_size], "col", -1)
    extended = jnp.concatenate([extended_rows, right_rim], axis=2)
    top_base = row_pos * tile_rows
    left_base = col_pos * tile_cols
    top_rows = positions[:, 0] - top_base
    left_cols = positions[:, 1] - left_base
    cosine_table, sine_table = dft_tables(patch_size)
    accumulator = jnp.zeros_like(extended)
    probe_sum = jnp.zeros_like(probe_field)
    window_shape = (2, patch_size, patch_size)

    def add_window(target, object_term, top_row, left_col):
        current = lax.dynamic_slice(target, (zero_index, top_row, left_col), window_shape)
        return lax.dynamic_update_slice(
            target, current + object_term, (zero_index, top_row, left_col)
        )

    def visit_slot(slot_index, loop_state):
        accum_now, probe_now = loop_state
        top_row = top_rows[slot_index]
        left_col = left_cols[slot_index]
        object_patch = lax.dynamic_slice(extended, (zero_index, top_row, left_col), window_shape)
        object_term, probe_term = exit_update(
            object_patch, probe_field, measured[slot_index], cosine_table, sine_table
        )
        return (add_window(accum_now, object_term, top_row, left_col), probe_now + probe_term)

    accumulator, probe_sum = lax.fori_loop(
        jnp.int32(0), counts[own_device], visit_slot, (accumulator, probe_sum)
    )
    right_back = passed_along(accumulator[:, :, tile_cols:], "col", 1)
    merged = jnp.concatenate(
        [accumulator[:, :, :patch_size] + right_back, accumulator[:, :, patch_size:tile_cols]],
        axis=2,
    )
    lower_back = passed_along(merged[:, tile_rows:, :], "row", 1)
    interior = jnp.concatenate(
        [merged[:, :patch_size, :] + lower_back, merged[:, patch_size:tile_rows, :]], axis=1
    )
    probe_total = lax.psum(probe_sum, ("row", "col"))
    live_total = jnp.sum(counts).astype(jnp.float32)
    new_object = object_field + OBJECT_RATE * interior
    new_probe = probe_field + probe_total / jnp.sqrt(live_total)
    return (new_object, new_probe)


def solution(mesh):
    placed = (
        P(None, "row", "col"),
        P(),
        P(("row", "col"), None, None),
        P(("row", "col"), None),
        P(),
    )
    return jax.shard_map(
        per_device,
        mesh=mesh,
        in_specs=placed,
        out_specs=(P(None, "row", "col"), P()),
        check_vma=False,
    )
```

profile of v0, /device:TPU:1, one launch (start us, length us, event | category | flops | bytes accessed | tf_op | source)
XLA Modules:
  0.0 937.4 jit_solution(14535646965015004309)
XLA Ops:
  8.7 3.3 collective-permute-start
  12.2 13.8 %collective-permute-done = f32[2,256,512]{2,1,0:T(8,128)S(1)} collective-permute-done((f32[2,256,512]{2,1,0:T(8,128)S(1)}, f32[2,256,512]{2,1,0:T(8,128)S(1)}, u32[]{:S(2)}, u32[]{:S(2)}) %collective-permute-start) | collective-permute-done | bytes 1048608 | tf_op jit(solution)/shard_map/ppermute | solution.py:15
  26.0 1.6 copy-done.4
  30.8 25.5 %collective-permute-done.1 = f32[2,768,256]{2,1,0:T(8,128)S(1)} collective-permute-done((f32[2,768,256]{2,1,0:T(8,128)}, f32[2,768,256]{2,1,0:T(8,128)S(1)}, u32[]{:S(2)}, u32[]{:S(2)}) %collective-permute-start.1) | collective-permute-done | bytes 1572896 | tf_op jit(solution)/shard_map/ppermute | solution.py:15
  56.3 4.4 pad_maximum_fusion
  60.7 2.5 broadcast_in_dim.6
  63.3 83.1 %while.14 = (s32[]{:T(128)}, f32[2,768,768]{2,1,0:T(8,128)}, f32[2,256,256]{2,1,0:T(8,128)S(1)}, s32[]{:T(128)}, s32[16]{0:T(128)S(1)}, /*index=5*/s32[16]{0:T(1...) while((s32[]{:T(128)}, f32[2,768,768]{2,1,0:T(8,128)}, ...), condition=%wide.region_1.2_spmd.clone.clone, body=%wide.region_0.1_spmd.clone.clone.sunk | while | flops 3239772160 | bytes 19661112 | solution.py:100
  80.6 2.5 fusion.178
  93.5 2.7 add_bitcast_fusion.2
  96.2 1.5 maximum_add_fusion.3
  97.7 6.8 dynamic_update_slice.6
  121.9 2.5 fusion.178
  134.8 2.7 add_bitcast_fusion.2
  137.5 1.5 maximum_add_fusion.3
  139.0 6.8 dynamic_update_slice.6
  146.4 1.7 slice.47
  148.1 249.7 %collective-permute-start.2 = (f32[2,768,256]{2,1,0:T(8,128)S(1)}, f32[2,768,256]{2,1,0:T(8,128)S(1)}, u32[]{:S(2)}, u32[]{:S(2)}) collective-permute-start(f32[2,768,256]{2,1,0:T(8,128)S(1)} %slice.47), channel_id=1, source_target_pairs={{0,1},{1,2},{2,3},{3,4},{4,5},{5,6},{6,7},{7,8},{8,9},{9,10},{10,1... | collective-permute-start | bytes 4718600 | tf_op jit(solution)/shard_map/ppermute | solution.py:15
  397.8 17.2 %collective-permute-done.2 = f32[2,768,256]{2,1,0:T(8,128)S(1)} collective-permute-done((f32[2,768,256]{2,1,0:T(8,128)S(1)}, f32[2,768,256]{2,1,0:T(8,128)S(1)}, u32[]{:S(2)}, u32[]{:S(2)}) %collective-permute-start.2) | collective-permute-done | bytes 1572896 | tf_op jit(solution)/shard_map/ppermute | solution.py:15
  415.1 2.2 slice_add_fusion
  418.8 342.3 %collective-permute-start.3 = (f32[2,256,512]{2,1,0:T(8,128)}, f32[2,256,512]{2,1,0:T(8,128)}, u32[]{:S(2)}, u32[]{:S(2)}) collective-permute-start(f32[2,256,512]{2,1,0:T(8,128)} %fusion.111), channel_id=1, source_target_pairs={{0,16},{16,32},{32,48},{48,64},{64,80},{80,96},{96,112},{1,17},{17... | collective-permute-start | bytes 3145736 | tf_op jit(solution)/shard_map/ppermute | solution.py:15
  762.5 162.4 %all-reduce.2.cloned.1.call-done = f32[2,256,256]{2,1,0:T(8,128)} async-done(((f32[2,256,256]{2,1,0:T(8,128)}), f32[2,256,256]{2,1,0:T(8,128)}) %all-reduce.2.cloned.1.call-update) | async-done | bytes 524304 | tf_op jit(solution)/shard_map/psum | solution.py:112
  924.9 2.0 divide_add_fusion
  927.0 1.5 fusion.113
  928.9 1.7 fusion.110
  (64 shorter events, 53.8 us)
Async XLA Ops:
  7.2 4.8 copy-start.5
  7.2 917.7 %all-reduce.2.cloned.1.call-start = ((), (), s32[]{:S(2)}) async-start(), calls=%async_computation | async-start | bytes 1048576 | tf_op jit(solution)/shard_map/psum | solution.py:112
  8.7 17.3 %collective-permute-start = (f32[2,256,512]{2,1,0:T(8,128)S(1)}, f32[2,256,512]{2,1,0:T(8,128)S(1)}, u32[]{:S(2)}, u32[]{:S(2)}) collective-permute-start(f32[2,256,512]{2,1,0:T(8,128)S(1)} %slice.44), channel_id=1, source_target_pairs={{16,0},{32,16},{48,32},{64,48},{80,64},{96,80},{112,96},{17,1},{33... | collective-permute-start | bytes 3145736 | tf_op jit(solution)/shard_map/ppermute | solution.py:15
  26.0 1.6 copy-start.4
  27.6 2.6 copy-start.8
  27.6 3.2 copy-start.7
  29.0 27.4 %collective-permute-start.1 = (f32[2,768,256]{2,1,0:T(8,128)}, f32[2,768,256]{2,1,0:T(8,128)S(1)}, u32[]{:S(2)}, u32[]{:S(2)}) collective-permute-start(f32[2,768,256]{2,1,0:T(8,128)} %slice.60), channel_id=1, source_target_pairs={{1,0},{2,1},{3,2},{4,3},{5,4},{6,5},{7,6},{8,7},{9,8},{10,9},{11,1... | collective-permute-start | bytes 4718600 | tf_op jit(solution)/shard_map/ppermute | solution.py:15
  60.7 2.5 copy-start
  146.4 270.9 %copy-start.1 = (f32[2,256,256]{2,1,0:T(8,128)}, f32[2,256,256]{2,1,0:T(8,128)S(1)}, u32[]{:S(2)}) copy-start(f32[2,256,256]{2,1,0:T(8,128)S(1)} %get-tuple-element.104) | copy-start | bytes 1572868
  148.1 267.0 %collective-permute-start.2 = (f32[2,768,256]{2,1,0:T(8,128)S(1)}, f32[2,768,256]{2,1,0:T(8,128)S(1)}, u32[]{:S(2)}, u32[]{:S(2)}) collective-permute-start(f32[2,768,256]{2,1,0:T(8,128)S(1)} %slice.47), channel_id=1, source_target_pairs={{0,1},{1,2},{2,3},{3,4},{4,5},{5,6},{6,7},{7,8},{8,9},{9,10},{10,1... | collective-permute-start | bytes 4718600 | tf_op jit(solution)/shard_map/ppermute | solution.py:15
  417.3 1.5 copy-start.2
  418.8 508.2 %collective-permute-start.3 = (f32[2,256,512]{2,1,0:T(8,128)}, f32[2,256,512]{2,1,0:T(8,128)}, u32[]{:S(2)}, u32[]{:S(2)}) collective-permute-start(f32[2,256,512]{2,1,0:T(8,128)} %fusion.111), channel_id=1, source_target_pairs={{0,16},{16,32},{32,48},{48,64},{64,80},{80,96},{96,112},{1,17},{17... | collective-permute-start | bytes 3145736 | tf_op jit(solution)/shard_map/ppermute | solution.py:15
  924.9 2.0 copy-start.3
  926.9 1.9 copy-start.6
Sparse Core Ops, SparseCore 0:
  761.3 163.6 all-reduce.1
where the time goes:
time: 943 us; the launch traced here: 937 us
  starting transfers between devices  597 us (63%)
  waiting for transfers between devices  219 us (23%)
  matrix products  51.7 us (5%)
  local copies, waits for them, and re-layouts  25.9 us (3%)
  other arithmetic  19.5 us (2%)
  between operations  14.9 us (2%)
  loops' own time  9.73 us (1%)
    ppermute x4, starting transfers between devices, passed_along(): return lax.ppermute(shard, axis, pairs)  597 us
    psum x1, waiting for transfers between devices, per_device(): probe_total = lax.psum(probe_sum, ('row', 'col'))  162 us
    ppermute x4, waiting for transfers between devices, passed_along(): return lax.ppermute(shard, axis, pairs)  56.5 us
    dot_general x32, matrix products, matmul(): jnp.dot(left_side, right_side, precision=lax.Precision.HIGHEST, preferred...  51.7 us
  transfers between devices with their start and end apart: 5, of which 4 were waited for; matrix products, arithmetic and copies ran while one was open for 0% of the time, Pallas kernels for 0%

commit v1 on v0

v1 whole, which is shorter than its diff:
```python
import functools
import math

import jax
import jax.numpy as jnp
import numpy as np
from jax import lax
from jax.experimental import pallas as pl
from jax.experimental.pallas import tpu as pltpu
from jax.sharding import PartitionSpec as P

FLOOR_SQUARED = 0.25 * 0.25
OBJECT_RATE = 0.5
PIX = 256
HALF = 128
ROWS = 16
F32 = jnp.float32
BF16 = jnp.bfloat16


def split_table(table):
    high = table.astype(jnp.bfloat16)
    low = (table - high.astype(np.float64)).astype(jnp.bfloat16)
    return high, low


def dft_tables():
    freq = np.arange(HALF)[:, None]
    place = np.arange(HALF)[None, :]
    left, right = [], []
    for inverse in (False, True):
        for odd in (0, 1):
            angle = -2.0 * math.pi * (((2 * freq + odd) * place) % PIX) / PIX
            real, imag = np.cos(angle) / 16.0, np.sin(angle) / 16.0
            whole = np.block([[real, -imag], [imag, real]])
            if inverse:
                whole = whole.T
            high, low = split_table(whole)
            left.append(np.concatenate([high, high, low], axis=1))
            high, low = split_table(whole.T)
            right.append(np.concatenate([high, high, low], axis=0))
    return np.stack(left), np.stack(right)


def permute_kernel(first_ref, second_ref, out_ref):
    lane = lax.broadcasted_iota(jnp.int32, (HALF, HALF), 1)
    first = lane < 64
    even_first = jnp.where(first, 2 * lane, 2 * lane - 127)
    odd_first = jnp.where(first, 2 * lane + 1, 2 * lane - 128)
    for parity in range(2):
        rows = pl.ds(parity, HALF, stride=2)
        left = jnp.take_along_axis(first_ref[0, rows, :], even_first, axis=1)
        right = jnp.take_along_axis(second_ref[0, rows, :], odd_first, axis=1)
        out_ref[0, parity * HALF : (parity + 1) * HALF, :HALF] = jnp.where(first, left, right)
        out_ref[0, parity * HALF : (parity + 1) * HALF, HALF:] = pltpu.roll(
            jnp.where(first, right, left), 64, 1
        )


def permuted(measured):
    slots = measured.shape[0]
    return pl.pallas_call(
        permute_kernel,
        grid=(slots,),
        in_specs=[pl.BlockSpec((1, PIX, HALF), lambda s, t=t: (s, 0, t)) for t in range(2)],
        out_specs=pl.BlockSpec((1, PIX, PIX), lambda s: (s, 0, 0)),
        out_shape=jax.ShapeDtypeStruct(measured.shape, F32),
        cost_estimate=pl.CostEstimate(flops=0, bytes_accessed=2 * measured.size * 4, transcendentals=0),
        name="permute_measured",
    )(measured, measured)


def slot_kernel(
    pairs,
    count_ref, top_ref, left_ref,
    object_ref, right_ref, lower_ref, corner_ref, probe_ref, measured_ref, left_tab, right_tab,
    interior_out, right_out, lower_out, probe_out,
    ext, acc, probe2, pacc, patch, probe_r, stack, lanes, spec_e, spec_o, sems,
):
    copies = [
        pltpu.make_async_copy(object_ref, ext.at[:, 0:512, 0:512], sems.at[0]),
        pltpu.make_async_copy(right_ref, ext.at[:, 0:512, 512:768], sems.at[1]),
        pltpu.make_async_copy(lower_ref, ext.at[:, 512:768, 0:512], sems.at[2]),
        pltpu.make_async_copy(corner_ref, ext.at[:, 512:768, 512:768], sems.at[3]),
    ]
    for copy in copies:
        copy.start()
    acc[...] = jnp.zeros_like(acc)
    pacc[...] = jnp.zeros_like(pacc)
    for plane in range(2):
        for tile in range(2):
            value = probe_ref[plane, :, tile * HALF : (tile + 1) * HALF]
            probe2[plane, tile, 0:PIX, :] = value
            probe2[plane, tile, PIX : 2 * PIX, :] = value
    for copy in copies:
        copy.wait()
    count = count_ref[0]
    lane = lax.broadcasted_iota(jnp.int32, (ROWS, HALF), 1)
    sub = lax.broadcasted_iota(jnp.int32, (ROWS, HALF), 0)

    def split(value):
        high = value.astype(BF16)
        return high, (value - high.astype(F32)).astype(BF16)

    def body(step, carry):
        group = []
        for p in range(pairs):
            index = step * pairs + p
            live = index < count
            index = jnp.minimum(index, 15)
            top, left = top_ref[index], left_ref[index]
            group.append(dict(
                p=p, index=index, live=live,
                m_r=top // PIX, s_r=top % PIX, m_c=left // PIX, s_c=left % PIX,
            ))

        for g in group:
            p, s_r, s_c = g["p"], g["s_r"], g["s_c"]
            swap, turn = s_c // HALF, s_c % HALF
            for i in range(HALF // ROWS):
                pieces = {}
                for half in range(2):
                    base = half * HALF + i * ROWS
                    row_far = sub + base < s_r
                    planes = []
                    for plane in range(2):
                        tiles = []
                        rolled = [
                            pltpu.roll(probe2[plane, (t + swap) % 2, pl.ds(PIX - s_r + base, ROWS), :], turn, 1)
                            for t in range(2)
                        ]
                        for t in range(2):
                            col_far = lane + t * HALF < s_c
                            blocks = [
                                [
                                    ext[
                                        plane,
                                        pl.ds(pl.multiple_of((g["m_r"] + dr) * PIX + base, ROWS), ROWS),
                                        pl.ds(pl.multiple_of((g["m_c"] + dc) * PIX + t * HALF, HALF), HALF),
                                    ]
                                    for dc in range(2)
                                ]
                                for dr in range(2)
                            ]
                            near = jnp.where(col_far, blocks[0][1], blocks[0][0])
                            far = jnp.where(col_far, blocks[1][1], blocks[1][0])
                            window = jnp.where(row_far, far, near)
                            patch[p, plane, base : base + ROWS, t * HALF : (t + 1) * HALF] = window
                            q = jnp.where(lane < turn, rolled[1 - t], rolled[t])
                            probe_r[p, plane, base : base + ROWS, t * HALF : (t + 1) * HALF] = q
                            tiles.append((window, q))
                        planes.append(tiles)
                    for t in range(2):
                        (o_re, q_re), (o_im, q_im) = planes[0][t], planes[1][t]
                        pieces[half, t] = (q_re * o_re - q_im * o_im, q_re * o_im + q_im * o_re)
                for t in range(2):
                    for c in range(2):
                        upper, under = pieces[0, t][c], pieces[1, t][c]
                        for j, value in enumerate((upper + under, upper - under)):
                            high, low = split(value)
                            r = c * HALF + i * ROWS
                            stack[p, j, r : r + ROWS, t * HALF : (t + 1) * HALF] = low
                            stack[p, j, PIX + r : PIX + r + ROWS, t * HALF : (t + 1) * HALF] = high

        def left_product(p, j, table):
            both = stack[p, j]
            value = jnp.concatenate([both, both[PIX:]], axis=0)
            return jnp.dot(left_tab[table], value, preferred_element_type=F32)

        def right_product(p, j, table):
            both = lanes[p, j]
            value = jnp.concatenate([both, both[:, PIX:]], axis=1)
            return jnp.dot(value, right_tab[table], preferred_element_type=F32)

        for g in group:
            p = g["p"]
            spec_e[p] = left_product(p, 0, 0)
            spec_o[p] = left_product(p, 1, 1)
        for g in group:
            p = g["p"]
            for half, source in enumerate((spec_e, spec_o)):
                for i in range(HALF // ROWS):
                    r = half * HALF + i * ROWS
                    for c in range(2):
                        s = c * HALF + i * ROWS
                        first = source[p, s : s + ROWS, :HALF]
                        second = source[p, s : s + ROWS, HALF:]
                        for j, value in enumerate((first + second, first - second)):
                            high, low = split(value)
                            lanes[p, j, r : r + ROWS, c * HALF : (c + 1) * HALF] = low
                            lanes[p, j, r : r + ROWS, PIX + c * HALF : PIX + (c + 1) * HALF] = high
        for g in group:
            p = g["p"]
            spec_e[p] = right_product(p, 0, 0)
            spec_o[p] = right_product(p, 1, 1)
        for g in group:
            p = g["p"]
            for j, source in enumerate((spec_e, spec_o)):
                for i in range(PIX // ROWS):
                    r = i * ROWS
                    re = source[p, r : r + ROWS, :HALF]
                    im = source[p, r : r + ROWS, HALF:]
                    amplitude = measured_ref[g["index"], r : r + ROWS, j * HALF : (j + 1) * HALF]
                    factor = amplitude * lax.rsqrt(jnp.maximum(re * re + im * im, FLOOR_SQUARED))
                    for c, value in enumerate((re * factor, im * factor)):
                        high, low = split(value)
                        lanes[p, j, r : r + ROWS, c * HALF : (c + 1) * HALF] = low
                        lanes[p, j, r : r + ROWS, PIX + c * HALF : PIX + (c + 1) * HALF] = high
        for g in group:
            p = g["p"]
            spec_e[p] = right_product(p, 0, 2)
            spec_o[p] = right_product(p, 1, 3)
        for g in group:
            p = g["p"]
            for j in range(2):
                for i in range(HALF // ROWS):
                    r = j * HALF + i * ROWS
                    for c in range(2):
                        first = spec_e[p, r : r + ROWS, c * HALF : (c + 1) * HALF]
                        second = spec_o[p, r : r + ROWS, c * HALF : (c + 1) * HALF]
                        for t, value in enumerate((first + second, first - second)):
                            high, low = split(value)
                            s = c * HALF + i * ROWS
                            stack[p, j, s : s + ROWS, t * HALF : (t + 1) * HALF] = low
                            stack[p, j, PIX + s : PIX + s + ROWS, t * HALF : (t + 1) * HALF] = high
        for g in group:
            p = g["p"]
            spec_e[p] = left_product(p, 0, 2)
            spec_o[p] = left_product(p, 1, 3)
        for g in group:
            p, s_r, s_c = g["p"], g["s_r"], g["s_c"]
            back = (PIX - s_c) % PIX
            swap, turn = back // HALF, back % HALF
            for i in range(HALF // ROWS):
                for half in range(2):
                    base = half * HALF + i * ROWS
                    row_far = sub + base < s_r
                    probe_terms = []
                    for t in range(2):
                        at = (slice(base, base + ROWS), slice(t * HALF, (t + 1) * HALF))
                        col_far = lane + t * HALF < s_c
                        o_re, o_im = patch[(p, 0) + at], patch[(p, 1) + at]
                        q_re, q_im = probe_r[(p, 0) + at], probe_r[(p, 1) + at]
                        diff = []
                        for c in range(2):
                            s = c * HALF + i * ROWS
                            first = spec_e[p, s : s + ROWS, t * HALF : (t + 1) * HALF]
                            second = spec_o[p, s : s + ROWS, t * HALF : (t + 1) * HALF]
                            diff.append(first + second if half == 0 else first - second)
                        d_re = diff[0] - (q_re * o_re - q_im * o_im)
                        d_im = diff[1] - (q_re * o_im + q_im * o_re)
                        d_re = jnp.where(g["live"], d_re, 0.0)
                        d_im = jnp.where(g["live"], d_im, 0.0)
                        terms = (q_re * d_re + q_im * d_im, q_re * d_im - q_im * d_re)
                        probe_terms.append((o_re * d_re + o_im * d_im, o_re * d_im - o_im * d_re))
                        for plane in range(2):
                            for dr in range(2):
                                for dc in range(2):
                                    mine = (row_far if dr else ~row_far) & (col_far if dc else ~col_far)
                                    spot = (
                                        plane,
                                        pl.ds(pl.multiple_of((g["m_r"] + dr) * PIX + base, ROWS), ROWS),
                                        pl.ds(pl.multiple_of((g["m_c"] + dc) * PIX + t * HALF, HALF), HALF),
                                    )
                                    acc[spot] += jnp.where(mine, terms[plane], 0.0)
                    for plane in range(2):
                        rolled = [pltpu.roll(probe_terms[t][plane], turn, 1) for t in range(2)]
                        for t in range(2):
                            value = jnp.where(lane < turn, rolled[1 - t], rolled[t])
                            spot = (plane, (t + swap) % 2, pl.ds(PIX - s_r + base, ROWS), slice(None))
                            pacc[spot] += value
        return carry

    lax.fori_loop(0, (count + pairs - 1) // pairs, body, jnp.int32(0))
    for plane in range(2):
        for tile in range(2):
            probe_out[plane, :, tile * HALF : (tile + 1) * HALF] = (
                pacc[plane, tile, 0:PIX, :] + pacc[plane, tile, PIX : 2 * PIX, :]
            )
    interior_out[...] = ext[:, 0:512, 0:512] + OBJECT_RATE * acc[:, 0:512, 0:512]
    right_out[...] = acc[:, :, 512:768]
    lower_out[...] = acc[:, 512:768, 0:512]


def process(count, tops, lefts, tile, right, lower, corner, probe, measured):
    left_tab, right_tab = dft_tables()
    pairs = 2
    vmem = pl.BlockSpec(memory_space=pltpu.VMEM)
    smem = pl.BlockSpec(memory_space=pltpu.SMEM)
    anywhere = pl.BlockSpec(memory_space=pl.ANY)
    return pl.pallas_call(
        functools.partial(slot_kernel, pairs),
        in_specs=[smem] * 3 + [anywhere] * 4 + [vmem] * 4,
        out_specs=[vmem] * 4,
        out_shape=[
            jax.ShapeDtypeStruct((2, 512, 512), F32),
            jax.ShapeDtypeStruct((2, 768, 256), F32),
            jax.ShapeDtypeStruct((2, 256, 512), F32),
            jax.ShapeDtypeStruct((2, 256, 256), F32),
        ],
        scratch_shapes=[
            pltpu.VMEM((2, 768, 768), F32),
            pltpu.VMEM((2, 768, 768), F32),
            pltpu.VMEM((2, 2, 512, HALF), F32),
            pltpu.VMEM((2, 2, 512, HALF), F32),
            pltpu.VMEM((pairs, 2, PIX, PIX), F32),
            pltpu.VMEM((pairs, 2, PIX, PIX), F32),
            pltpu.VMEM((pairs, 2, 2 * PIX, PIX), BF16),
            pltpu.VMEM((pairs, 2, PIX, 2 * PIX), BF16),
            pltpu.VMEM((pairs, PIX, PIX), F32),
            pltpu.VMEM((pairs, PIX, PIX), F32),
            pltpu.SemaphoreType.DMA((4,)),
        ],
        compiler_params=pltpu.CompilerParams(vmem_limit_bytes=56 * 1024 * 1024),
        cost_estimate=pl.CostEstimate(flops=13 * 10**9, bytes_accessed=12 * 2**20, transcendentals=2**20),
        name="slots",
    )(count, tops, lefts, tile, right, lower, corner, probe, measured, jnp.asarray(left_tab), jnp.asarray(right_tab))


def passed_along(shard, axis, by):
    peers = lax.axis_size(axis)
    pairs = [(i, i + by) for i in range(peers) if 0 <= i + by < peers]
    return lax.ppermute(shard, axis, pairs)


def per_device(object_field, probe_field, measured, positions, counts):
    row_pos = lax.axis_index("row")
    col_pos = lax.axis_index("col")
    own_device = row_pos * lax.axis_size("col") + col_pos
    lower = passed_along(object_field[:, :PIX, :], "row", -1)
    right = passed_along(object_field[:, :, :PIX], "col", -1)
    corner = passed_along(right[:, :PIX, :], "row", -1)
    ordered = permuted(measured)
    tops = positions[:, 0] - row_pos * 512
    lefts = positions[:, 1] - col_pos * 512
    count = counts[own_device][None]
    interior, right_sum, lower_sum, probe_sum = process(
        count, tops, lefts, object_field, right, lower, corner, probe_field, ordered
    )
    probe_total = probe_reduced(probe_sum)
    corner_back = passed_along(right_sum[:, 512:], "row", 1)
    lower_back = passed_along(lower_sum, "row", 1)
    top_right = right_sum[:, :PIX] + corner_back
    top_back = passed_along(top_right, "col", 1)
    bottom_back = passed_along(right_sum[:, PIX:512], "col", 1)
    new_object = interior
    new_object = new_object.at[:, :PIX, :].add(OBJECT_RATE * lower_back)
    new_object = new_object.at[:, :PIX, :PIX].add(OBJECT_RATE * top_back)
    new_object = new_object.at[:, PIX:, :PIX].add(OBJECT_RATE * bottom_back)
    live_total = jnp.sum(counts).astype(F32)
    new_probe = probe_field + probe_total / jnp.sqrt(live_total)
    return (new_object, new_probe)


def probe_reduced(value):
    shape = value.shape
    core = lax.axis_index("row") % 2
    x_pos = lax.axis_index("row") // 2

    def over_core(v):
        return lax.ppermute(v, "row", [(i, i ^ 1) for i in range(8)])

    def over_x(v, k):
        return lax.ppermute(v, "row", [(i, (i + 2 * k) % 8) for i in range(8)])

    def over_y(v, k):
        return lax.ppermute(v, "col", [(i, (i + 4 * k) % 16) for i in range(16)])

    def over_z(v, k):
        return lax.ppermute(v, "col", [(i, i // 4 * 4 + (i % 4 + k) % 4) for i in range(16)])

    def pick(v, i):
        return lax.dynamic_index_in_dim(v, i, 0, False)

    halves = value.reshape(2, 512, 128)
    mine = pick(halves, core) + over_core(pick(halves, 1 - core))
    quarters = mine.reshape(4, 128, 128)
    part = pick(quarters, x_pos)
    for k in (1, 2, 3):
        part = part + over_x(pick(quarters, (x_pos + k) % 4), k)
    part = (part + over_y(part, 2)) + (over_y(part, 1) + over_y(part, 3))
    part = (part + over_z(part, 2)) + (over_z(part, 1) + over_z(part, 3))
    whole = jnp.zeros((4, 128, 128), F32)
    whole = lax.dynamic_update_index_in_dim(whole, part, x_pos, 0)
    for k in (1, 2, 3):
        whole = lax.dynamic_update_index_in_dim(whole, over_x(part, k), (x_pos - k) % 4, 0)
    half = whole.reshape(512, 128)
    other = over_core(half)
    return jnp.concatenate(
        [jnp.where(core == 0, half, other), jnp.where(core == 0, other, half)], axis=0
    ).reshape(shape)


def solution(mesh):
    placed = (
        P(None, "row", "col"),
        P(),
        P(("row", "col"), None, None),
        P(("row", "col"), None),
        P(),
    )
    return jax.shard_map(
        per_device,
        mesh=mesh,
        in_specs=placed,
        out_specs=(P(None, "row", "col"), P()),
        check_vma=False,
    )
```

time: 943 us -> 166 us (0.18)
  starting transfers between devices: 597 us -> 77.4 us
  waiting for transfers between devices: 219 us -> 44.5 us
  matrix products: 51.7 us -> 0 us
  Pallas kernels: 0 us -> 25.2 us
  local copies, waits for them, and re-layouts: 25.9 us -> 6.91 us
  between operations: 14.9 us -> 1.65 us
  other arithmetic: 19.5 us -> 8.23 us
  loops' own time: 9.73 us -> 0 us
    ppermute x4 -> x7, starting transfers between devices: 597 us -> 21.3 us  [passed_along(): return lax.ppermute(shard, axis, pairs)]
    psum x1 -> x0, waiting for transfers between devices: 162 us -> none  [per_device(): probe_total = lax.psum(probe_sum, ('row', 'col'))]
    ppermute x0 -> x14, starting transfers between devices: none -> 56.2 us  [the longest x2 28.9 us: over_core(): return lax.ppermute(v, 'row', [(i, i ^ 1) for i in range(8)])]
    dot_general x32 -> x0, matrix products: 51.7 us -> none  [matmul(): jnp.dot(left_side, right_side, precision=lax.Precision.HIGHEST, preferred...]
    ppermute x4 -> x7, waiting for transfers between devices: 56.5 us -> 28.9 us  [passed_along(): return lax.ppermute(shard, axis, pairs)]
    pallas_call x0 -> x2, Pallas kernels: none -> 25.2 us  [the longest x1 13 us: process(): pl.pallas_call(functools.partial(slot_kernel, pairs), in_specs=[smem] * 3...]
    ppermute x0 -> x14, waiting for transfers between devices: none -> 15.6 us  [the longest x6 11.7 us: over_x(): return lax.ppermute(v, 'row', [(i, (i + 2 * k) % 8) for i in range(8)])]
    dynamic_update_slice x2 -> x3, local copies, waits for them, and re-layouts: 13.6 us -> 0.03 us  [probe_reduced(): lax.dynamic_update_index_in_dim(whole, over_x(part, k), (x_pos - k) % 4, 0)]
  transfers between devices with their start and end apart: 5 -> 21, of which waited for: 4 -> 10; matrix products, arithmetic and copies ran while one was open for 0% -> 5% of each run, Pallas kernels for 0% -> 7%
where the time goes in v1:
time: 166 us; the launch traced here: 164 us
  starting transfers between devices  77.4 us (47%)
  waiting for transfers between devices  44.5 us (27%)
  Pallas kernels  25.2 us (15%)
  other arithmetic  8.23 us (5%)
  local copies, waits for them, and re-layouts  6.91 us (4%)
    ppermute x7, waiting for transfers between devices, passed_along(): return lax.ppermute(shard, axis, pairs)  28.9 us
    ppermute x2, starting transfers between devices, over_core(): return lax.ppermute(v, 'row', [(i, i ^ 1) for i in range(8)])  28.9 us
    ppermute x7, starting transfers between devices, passed_along(): return lax.ppermute(shard, axis, pairs)  21.3 us
    ppermute x6, starting transfers between devices, over_x(): return lax.ppermute(v, 'row', [(i, (i + 2 * k) % 8) for i in range(8)])  13.1 us
    pallas_call x1, Pallas kernels, process(): pl.pallas_call(functools.partial(slot_kernel, pairs), in_specs=[smem] * 3...  13 us
    pallas_call x1, Pallas kernels, permuted(): pl.pallas_call(permute_kernel, grid=(slots,), in_specs=[pl.BlockSpec((1,...  12.2 us
    ppermute x6, waiting for transfers between devices, over_x(): return lax.ppermute(v, 'row', [(i, (i + 2 * k) % 8) for i in range(8)])  11.7 us
    ppermute x3, starting transfers between devices, over_y(): return lax.ppermute(v, 'col', [(i, (i + 4 * k) % 16) for i in range(16)])  7.1 us
  transfers between devices with their start and end apart: 21, of which 10 were waited for; matrix products, arithmetic and copies ran while one was open for 5% of the time, Pallas kernels for 7%

profile of v1, /device:TPU:1, one launch (start us, length us, event | category | flops | bytes accessed | tf_op | source)
XLA Modules:
  0.0 163.9 jit_solution(16508225822706973938)
XLA Ops:
  3.5 3.3 %collective-permute-start.1 = (f32[2,256,512]{2,1,0:T(8,128)S(1)}, f32[2,256,512]{2,1,0:T(8,128)S(1)}, u32[]{:S(2)}, u32[]{:S(2)}) collective-permute-start(f32[2,256,512]{2,1,0:T(8,128)S(1)} %slice.110), channel_id=1, source_target_pairs={{16,0},{32,16},{48,32},{64,48},{80,64},{96,80},{112,96},{17,1},{33... | collective-permute-start | bytes 3145736 | tf_op jit(solution)/shard_map/ppermute | solution.py:323
  6.8 22.5 %collective-permute-done.right_ref = f32[2,512,256]{2,1,0:T(8,128)S(1)} collective-permute-done((f32[2,512,256]{2,1,0:T(8,128)S(1)}, f32[2,512,256]{2,1,0:T(8,128)S(1)}, u32[]{:S(2)}, u32[]{:S(2)}) %collective-permute-start) | collective-permute-done | bytes 1048608 | tf_op jit(solution)/shard_map/ppermute | solution.py:323
  29.4 3.2 %collective-permute-start.2 = (f32[2,256,256]{2,1,0:T(8,128)S(1)}, f32[2,256,256]{2,1,0:T(8,128)}, u32[]{:S(2)}, u32[]{:S(2)}) collective-permute-start(f32[2,256,256]{2,1,0:T(8,128)S(1)} %slice.118), channel_id=1, source_target_pairs={{16,0},{32,16},{48,32},{64,48},{80,64},{96,80},{112,96},{17,1},{33... | collective-permute-start | bytes 1572872 | tf_op jit(solution)/shard_map/ppermute | solution.py:323
  32.6 12.2 %permute_measured.1.measured_ref = f32[16,256,256]{2,1,0:T(8,128)} custom-call(f32[16,256,256]{2,1,0:T(8,128)} %second_ref.1, f32[16,256,256]{2,1,0:T(8,128)} %second_ref.1), custom_call_target="tpu_custom_call" | custom-call | bytes 8388608 | tf_op jit(solution)/shard_map/permute_measured/pallas_call | solution.py:62
  47.0 13.0 %slots.1 = (f32[2,512,512]{2,1,0:T(8,128)}, f32[2,768,256]{2,1,0:T(8,128)}, f32[2,256,512]{2,1,0:T(8,128)}, f32[2,256,256]{2,1,0:T(8,128)}) custom-call(s32[1]{0:T(128)} %dynamic_slice.23.count_ref, s32[16]{0:T(128)} %get-tuple-element.58.top_ref, s32[16]{0:T(128)} %get-tuple-element.57.left_ref, f32[2,512,512]{2,1,0:T(8,128)} %object_ref.1, ...), custom_call_target="tpu_custom_call" | custom-call | flops 12999999488 | bytes 12582912 | tf_op jit(solution)/shard_map/slots/pallas_call | solution.py:291
  61.3 28.8 %collective-permute-start.7 = (f32[512,128]{1,0:T(8,128)S(1)}, f32[512,128]{1,0:T(8,128)S(1)}, u32[]{:S(2)}, u32[]{:S(2)}) collective-permute-start(f32[512,128]{1,0:T(8,128)S(1)} %dynamic-slice_bitcast_fusion), channel_id=1, source_target_pairs={{0,16},{16,0},{32,48},{48,32},{64,80},{80,64},{96,112},{112,96},{1... | collective-permute-start | bytes 786440 | tf_op jit(solution)/shard_map/ppermute | solution.py:361
  91.4 3.7 %collective-permute-start.9 = (f32[128,128]{1,0:T(8,128)S(1)}, f32[128,128]{1,0:T(8,128)S(1)}, u32[]{:S(2)}, u32[]{:S(2)}) collective-permute-start(f32[128,128]{1,0:T(8,128)S(1)} %get-tuple-element.56), channel_id=1, source_target_pairs={{0,64},{16,80},{32,96},{48,112},{64,0},{80,16},{96,32},{112,48},{1... | collective-permute-start | bytes 196616 | tf_op jit(solution)/shard_map/ppermute | solution.py:364
  96.7 2.7 %collective-permute-done.8 = f32[128,128]{1,0:T(8,128)S(1)} collective-permute-done((f32[128,128]{1,0:T(8,128)S(1)}, f32[128,128]{1,0:T(8,128)S(1)}, u32[]{:S(2)}, u32[]{:S(2)}) %collective-permute-start.8) | collective-permute-done | bytes 65568 | tf_op jit(solution)/shard_map/ppermute | solution.py:364
  99.4 5.2 %collective-permute-start.12 = (f32[128,128]{1,0:T(8,128)S(1)}, f32[128,128]{1,0:T(8,128)S(1)}, u32[]{:S(2)}, u32[]{:S(2)}) collective-permute-start(f32[128,128]{1,0:T(8,128)S(1)} %fusion.3), channel_id=1, source_target_pairs={{0,4},{1,5},{2,6},{3,7},{4,8},{5,9},{6,10},{7,11},{8,12},{9,13},{1... | collective-permute-start | bytes 196616 | tf_op jit(solution)/shard_map/ppermute | solution.py:367
  104.6 1.9 %collective-permute-start.11 = (f32[128,128]{1,0:T(8,128)S(1)}, f32[128,128]{1,0:T(8,128)S(1)}, u32[]{:S(2)}, u32[]{:S(2)}) collective-permute-start(f32[128,128]{1,0:T(8,128)S(1)} %fusion.3), channel_id=1, source_target_pairs={{0,8},{1,9},{2,10},{3,11},{4,12},{5,13},{6,14},{7,15},{8,0},{9,1},... | collective-permute-start | bytes 196616 | tf_op jit(solution)/shard_map/ppermute | solution.py:367
  107.7 1.5 collective-permute-done.11
  109.8 5.4 %collective-permute-start.16 = (f32[128,128]{1,0:T(8,128)S(1)}, f32[128,128]{1,0:T(8,128)S(1)}, u32[]{:S(2)}, u32[]{:S(2)}) collective-permute-start(f32[128,128]{1,0:T(8,128)S(1)} %add_add_fusion.1), channel_id=1, source_target_pairs={{0,3},{1,0},{2,1},{3,2},{4,7},{5,4},{6,5},{7,6},{8,11},{9,8},{10,9... | collective-permute-start | bytes 196616 | tf_op jit(solution)/shard_map/ppermute | solution.py:370
  117.7 3.6 %collective-permute-start.3 = (f32[2,256,512]{2,1,0:T(8,128)}, f32[2,256,512]{2,1,0:T(8,128)}, u32[]{:S(2)}, u32[]{:S(2)}) collective-permute-start(f32[2,256,512]{2,1,0:T(8,128)} %get-tuple-element.43), channel_id=1, source_target_pairs={{0,16},{16,32},{32,48},{48,64},{64,80},{80,96},{96,112},{1,17},{17... | collective-permute-start | bytes 3145736 | tf_op jit(solution)/shard_map/ppermute | solution.py:323
  121.4 1.8 %collective-permute-start.17 = (f32[128,128]{1,0:T(8,128)S(1)}, f32[128,128]{1,0:T(8,128)S(1)}, u32[]{:S(2)}, u32[]{:S(2)}) collective-permute-start(f32[128,128]{1,0:T(8,128)S(1)} %get-tuple-element.47), channel_id=1, source_target_pairs={{0,32},{16,48},{32,64},{48,80},{64,96},{80,112},{96,0},{112,16},{1... | collective-permute-start | bytes 196616 | tf_op jit(solution)/shard_map/ppermute | solution.py:364
  124.0 3.3 %collective-permute-start.4 = (f32[2,256,256]{2,1,0:T(8,128)S(1)}, f32[2,256,256]{2,1,0:T(8,128)S(1)}, u32[]{:S(2)}, u32[]{:S(2)}) collective-permute-start(f32[2,256,256]{2,1,0:T(8,128)S(1)} %get-tuple-element.51), channel_id=1, source_target_pairs={{0,16},{16,32},{32,48},{48,64},{64,80},{80,96},{96,112},{1,17},{17... | collective-permute-start | bytes 1572872 | tf_op jit(solution)/shard_map/ppermute | solution.py:323
  127.3 2.8 %collective-permute-start.6 = (f32[2,256,256]{2,1,0:T(8,128)}, f32[2,256,256]{2,1,0:T(8,128)}, u32[]{:S(2)}, u32[]{:S(2)}) collective-permute-start(f32[2,256,256]{2,1,0:T(8,128)} %get-tuple-element.50), channel_id=1, source_target_pairs={{0,1},{1,2},{2,3},{3,4},{4,5},{5,6},{6,7},{7,8},{8,9},{9,10},{10,1... | collective-permute-start | bytes 1572872 | tf_op jit(solution)/shard_map/ppermute | solution.py:323
  130.1 3.7 %collective-permute-start.18 = (f32[128,128]{1,0:T(8,128)S(1)}, f32[128,128]{1,0:T(8,128)S(1)}, u32[]{:S(2)}, u32[]{:S(2)}) collective-permute-start(f32[128,128]{1,0:T(8,128)S(1)} %get-tuple-element.47), channel_id=1, source_target_pairs={{0,64},{16,80},{32,96},{48,112},{64,0},{80,16},{96,32},{112,48},{1... | collective-permute-start | bytes 196616 | tf_op jit(solution)/shard_map/ppermute | solution.py:364
  133.8 1.6 collective-permute-done.17
  135.3 3.9 %collective-permute-start.19 = (f32[128,128]{1,0:T(8,128)S(1)}, f32[128,128]{1,0:T(8,128)S(1)}, u32[]{:S(2)}, u32[]{:S(2)}) collective-permute-start(f32[128,128]{1,0:T(8,128)S(1)} %get-tuple-element.47), channel_id=1, source_target_pairs={{0,96},{16,112},{32,0},{48,16},{64,32},{80,48},{96,64},{112,80},{1... | collective-permute-start | bytes 196616 | tf_op jit(solution)/shard_map/ppermute | solution.py:364
  139.3 5.8 %collective-permute-done.18 = f32[128,128]{1,0:T(8,128)S(1)} collective-permute-done((f32[128,128]{1,0:T(8,128)S(1)}, f32[128,128]{1,0:T(8,128)S(1)}, u32[]{:S(2)}, u32[]{:S(2)}) %collective-permute-start.18) | collective-permute-done | bytes 65568 | tf_op jit(solution)/shard_map/ppermute | solution.py:364
  146.1 3.8 %collective-permute-start.5 = (f32[2,256,256]{2,1,0:T(8,128)}, f32[2,256,256]{2,1,0:T(8,128)}, u32[]{:S(2)}, u32[]{:S(2)}) collective-permute-start(f32[2,256,256]{2,1,0:T(8,128)} %slice_add_fusion.2), channel_id=1, source_target_pairs={{0,1},{1,2},{2,3},{3,4},{4,5},{5,6},{6,7},{7,8},{8,9},{9,10},{10,1... | collective-permute-start | bytes 1572872 | tf_op jit(solution)/shard_map/ppermute | solution.py:323
  150.2 2.0 %add.165 = f32[2,256,256]{2,1,0:T(8,128)} add(f32[2,256,256]{2,1,0:T(8,128)} %probe_ref.1, f32[2,256,256]{2,1,0:T(8,128)S(1)} %div.22) | non-fusion elementwise | flops 131072 | bytes 1572864 | tf_op jit(solution)/shard_map/add | solution.py:351
  152.2 1.6 constant_dynamic-update-slice_fusion
  153.8 6.4 %collective-permute-done.5 = f32[2,256,256]{2,1,0:T(8,128)} collective-permute-done((f32[2,256,256]{2,1,0:T(8,128)}, f32[2,256,256]{2,1,0:T(8,128)}, u32[]{:S(2)}, u32[]{:S(2)}) %collective-permute-start.5) | collective-permute-done | bytes 524320 | tf_op jit(solution)/shard_map/ppermute | solution.py:323
  (62 shorter events, 18.7 us)
Async XLA Ops:
  2.1 27.2 %collective-permute-start = (f32[2,512,256]{2,1,0:T(8,128)S(1)}, f32[2,512,256]{2,1,0:T(8,128)S(1)}, u32[]{:S(2)}, u32[]{:S(2)}) collective-permute-start(f32[2,512,256]{2,1,0:T(8,128)S(1)} %slice.109), channel_id=1, source_target_pairs={{1,0},{2,1},{3,2},{4,3},{5,4},{6,5},{7,6},{8,7},{9,8},{10,9},{11,1... | collective-permute-start | bytes 3145736 | tf_op jit(solution)/shard_map/ppermute | solution.py:323
  3.5 42.5 %collective-permute-start.1 = (f32[2,256,512]{2,1,0:T(8,128)S(1)}, f32[2,256,512]{2,1,0:T(8,128)S(1)}, u32[]{:S(2)}, u32[]{:S(2)}) collective-permute-start(f32[2,256,512]{2,1,0:T(8,128)S(1)} %slice.110), channel_id=1, source_target_pairs={{16,0},{32,16},{48,32},{64,48},{80,64},{96,80},{112,96},{17,1},{33... | collective-permute-start | bytes 3145736 | tf_op jit(solution)/shard_map/ppermute | solution.py:323
  29.4 16.6 %collective-permute-start.2 = (f32[2,256,256]{2,1,0:T(8,128)S(1)}, f32[2,256,256]{2,1,0:T(8,128)}, u32[]{:S(2)}, u32[]{:S(2)}) collective-permute-start(f32[2,256,256]{2,1,0:T(8,128)S(1)} %slice.118), channel_id=1, source_target_pairs={{16,0},{32,16},{48,32},{64,48},{80,64},{96,80},{112,96},{17,1},{33... | collective-permute-start | bytes 1572872 | tf_op jit(solution)/shard_map/ppermute | solution.py:323
  32.5 12.2 %copy-start.7 = (s32[128]{0:T(128)S(1)}, s32[128]{0:T(128)}, u32[]{:S(2)}) copy-start(s32[128]{0:T(128)} %param.17) | copy-start | bytes 1540
  32.6 12.9 %copy-start.5 = (s32[16,2]{0,1:T(2,128)S(1)}, s32[16,2]{0,1:T(2,128)}, u32[]{:S(2)}) copy-start(s32[16,2]{0,1:T(2,128)} %param.16) | copy-start | bytes 388
  60.0 63.2 %copy-start.1 = (f32[2,768,256]{2,1,0:T(8,128)S(1)}, f32[2,768,256]{2,1,0:T(8,128)}, u32[]{:S(2)}) copy-start(f32[2,768,256]{2,1,0:T(8,128)} %get-tuple-element.44) | copy-start | bytes 4718596
  61.3 30.0 %collective-permute-start.7 = (f32[512,128]{1,0:T(8,128)S(1)}, f32[512,128]{1,0:T(8,128)S(1)}, u32[]{:S(2)}, u32[]{:S(2)}) collective-permute-start(f32[512,128]{1,0:T(8,128)S(1)} %dynamic-slice_bitcast_fusion), channel_id=1, source_target_pairs={{0,16},{16,0},{32,48},{48,32},{64,80},{80,64},{96,112},{112,96},{1... | collective-permute-start | bytes 786440 | tf_op jit(solution)/shard_map/ppermute | solution.py:361
  91.3 4.1 %collective-permute-start.10 = (f32[128,128]{1,0:T(8,128)S(1)}, f32[128,128]{1,0:T(8,128)S(1)}, u32[]{:S(2)}, u32[]{:S(2)}) collective-permute-start(f32[128,128]{1,0:T(8,128)S(1)} %get-tuple-element.55), channel_id=1, source_target_pairs={{0,96},{16,112},{32,0},{48,16},{64,32},{80,48},{96,64},{112,80},{1... | collective-permute-start | bytes 196616 | tf_op jit(solution)/shard_map/ppermute | solution.py:364
  91.4 5.3 %collective-permute-start.9 = (f32[128,128]{1,0:T(8,128)S(1)}, f32[128,128]{1,0:T(8,128)S(1)}, u32[]{:S(2)}, u32[]{:S(2)}) collective-permute-start(f32[128,128]{1,0:T(8,128)S(1)} %get-tuple-element.56), channel_id=1, source_target_pairs={{0,64},{16,80},{32,96},{48,112},{64,0},{80,16},{96,32},{112,48},{1... | collective-permute-start | bytes 196616 | tf_op jit(solution)/shard_map/ppermute | solution.py:364
  95.0 4.3 %collective-permute-start.8 = (f32[128,128]{1,0:T(8,128)S(1)}, f32[128,128]{1,0:T(8,128)S(1)}, u32[]{:S(2)}, u32[]{:S(2)}) collective-permute-start(f32[128,128]{1,0:T(8,128)S(1)} %get-tuple-element.54), channel_id=1, source_target_pairs={{0,32},{16,48},{32,64},{48,80},{64,96},{80,112},{96,0},{112,16},{1... | collective-permute-start | bytes 196616 | tf_op jit(solution)/shard_map/ppermute | solution.py:364
  99.4 7.1 %collective-permute-start.12 = (f32[128,128]{1,0:T(8,128)S(1)}, f32[128,128]{1,0:T(8,128)S(1)}, u32[]{:S(2)}, u32[]{:S(2)}) collective-permute-start(f32[128,128]{1,0:T(8,128)S(1)} %fusion.3), channel_id=1, source_target_pairs={{0,4},{1,5},{2,6},{3,7},{4,8},{5,9},{6,10},{7,11},{8,12},{9,13},{1... | collective-permute-start | bytes 196616 | tf_op jit(solution)/shard_map/ppermute | solution.py:367
  104.6 3.1 %collective-permute-start.13 = (f32[128,128]{1,0:T(8,128)S(1)}, f32[128,128]{1,0:T(8,128)S(1)}, u32[]{:S(2)}, u32[]{:S(2)}) collective-permute-start(f32[128,128]{1,0:T(8,128)S(1)} %fusion.3), channel_id=1, source_target_pairs={{0,12},{1,13},{2,14},{3,15},{4,0},{5,1},{6,2},{7,3},{8,4},{9,5},{1... | collective-permute-start | bytes 196616 | tf_op jit(solution)/shard_map/ppermute | solution.py:367
  104.6 4.6 %collective-permute-start.11 = (f32[128,128]{1,0:T(8,128)S(1)}, f32[128,128]{1,0:T(8,128)S(1)}, u32[]{:S(2)}, u32[]{:S(2)}) collective-permute-start(f32[128,128]{1,0:T(8,128)S(1)} %fusion.3), channel_id=1, source_target_pairs={{0,8},{1,9},{2,10},{3,11},{4,12},{5,13},{6,14},{7,15},{8,0},{9,1},... | collective-permute-start | bytes 196616 | tf_op jit(solution)/shard_map/ppermute | solution.py:367
  109.3 12.0 %collective-permute-start.15 = (f32[128,128]{1,0:T(8,128)S(1)}, f32[128,128]{1,0:T(8,128)S(1)}, u32[]{:S(2)}, u32[]{:S(2)}) collective-permute-start(f32[128,128]{1,0:T(8,128)S(1)} %add_add_fusion.1), channel_id=1, source_target_pairs={{0,1},{1,2},{2,3},{3,0},{4,5},{5,6},{6,7},{7,4},{8,9},{9,10},{10,1... | collective-permute-start | bytes 196616 | tf_op jit(solution)/shard_map/ppermute | solution.py:370
  109.8 11.5 %collective-permute-start.16 = (f32[128,128]{1,0:T(8,128)S(1)}, f32[128,128]{1,0:T(8,128)S(1)}, u32[]{:S(2)}, u32[]{:S(2)}) collective-permute-start(f32[128,128]{1,0:T(8,128)S(1)} %add_add_fusion.1), channel_id=1, source_target_pairs={{0,3},{1,0},{2,1},{3,2},{4,7},{5,4},{6,5},{7,6},{8,11},{9,8},{10,9... | collective-permute-start | bytes 196616 | tf_op jit(solution)/shard_map/ppermute | solution.py:370
  115.2 6.1 %collective-permute-start.14 = (f32[128,128]{1,0:T(8,128)S(1)}, f32[128,128]{1,0:T(8,128)S(1)}, u32[]{:S(2)}, u32[]{:S(2)}) collective-permute-start(f32[128,128]{1,0:T(8,128)S(1)} %add_add_fusion.1), channel_id=1, source_target_pairs={{0,2},{1,3},{2,0},{3,1},{4,6},{5,7},{6,4},{7,5},{8,10},{9,11},{10,... | collective-permute-start | bytes 196616 | tf_op jit(solution)/shard_map/ppermute | solution.py:370
  117.7 34.5 %collective-permute-start.3 = (f32[2,256,512]{2,1,0:T(8,128)}, f32[2,256,512]{2,1,0:T(8,128)}, u32[]{:S(2)}, u32[]{:S(2)}) collective-permute-start(f32[2,256,512]{2,1,0:T(8,128)} %get-tuple-element.43), channel_id=1, source_target_pairs={{0,16},{16,32},{32,48},{48,64},{64,80},{80,96},{96,112},{1,17},{17... | collective-permute-start | bytes 3145736 | tf_op jit(solution)/shard_map/ppermute | solution.py:323
  121.4 14.0 %collective-permute-start.17 = (f32[128,128]{1,0:T(8,128)S(1)}, f32[128,128]{1,0:T(8,128)S(1)}, u32[]{:S(2)}, u32[]{:S(2)}) collective-permute-start(f32[128,128]{1,0:T(8,128)S(1)} %get-tuple-element.47), channel_id=1, source_target_pairs={{0,32},{16,48},{32,64},{48,80},{64,96},{80,112},{96,0},{112,16},{1... | collective-permute-start | bytes 196616 | tf_op jit(solution)/shard_map/ppermute | solution.py:364
  124.0 21.2 %collective-permute-start.4 = (f32[2,256,256]{2,1,0:T(8,128)S(1)}, f32[2,256,256]{2,1,0:T(8,128)S(1)}, u32[]{:S(2)}, u32[]{:S(2)}) collective-permute-start(f32[2,256,256]{2,1,0:T(8,128)S(1)} %get-tuple-element.51), channel_id=1, source_target_pairs={{0,16},{16,32},{32,48},{48,64},{64,80},{80,96},{96,112},{1,17},{17... | collective-permute-start | bytes 1572872 | tf_op jit(solution)/shard_map/ppermute | solution.py:323
  127.3 34.1 %collective-permute-start.6 = (f32[2,256,256]{2,1,0:T(8,128)}, f32[2,256,256]{2,1,0:T(8,128)}, u32[]{:S(2)}, u32[]{:S(2)}) collective-permute-start(f32[2,256,256]{2,1,0:T(8,128)} %get-tuple-element.50), channel_id=1, source_target_pairs={{0,1},{1,2},{2,3},{3,4},{4,5},{5,6},{6,7},{7,8},{8,9},{9,10},{10,1... | collective-permute-start | bytes 1572872 | tf_op jit(solution)/shard_map/ppermute | solution.py:323
  130.1 15.0 %collective-permute-start.18 = (f32[128,128]{1,0:T(8,128)S(1)}, f32[128,128]{1,0:T(8,128)S(1)}, u32[]{:S(2)}, u32[]{:S(2)}) collective-permute-start(f32[128,128]{1,0:T(8,128)S(1)} %get-tuple-element.47), channel_id=1, source_target_pairs={{0,64},{16,80},{32,96},{48,112},{64,0},{80,16},{96,32},{112,48},{1... | collective-permute-start | bytes 196616 | tf_op jit(solution)/shard_map/ppermute | solution.py:364
  135.3 9.7 %collective-permute-start.19 = (f32[128,128]{1,0:T(8,128)S(1)}, f32[128,128]{1,0:T(8,128)S(1)}, u32[]{:S(2)}, u32[]{:S(2)}) collective-permute-start(f32[128,128]{1,0:T(8,128)S(1)} %get-tuple-element.47), channel_id=1, source_target_pairs={{0,96},{16,112},{32,0},{48,16},{64,32},{80,48},{96,64},{112,80},{1... | collective-permute-start | bytes 196616 | tf_op jit(solution)/shard_map/ppermute | solution.py:364
  145.1 4.8 %collective-permute-start.20 = (f32[512,128]{1,0:T(8,128)S(1)}, f32[512,128]{1,0:T(8,128)S(1)}, u32[]{:S(2)}, u32[]{:S(2)}) collective-permute-start(f32[512,128]{1,0:T(8,128)S(1)} %bitcast.34), channel_id=1, source_target_pairs={{0,16},{16,0},{32,48},{48,32},{64,80},{80,64},{96,112},{112,96},{1... | collective-permute-start | bytes 786440 | tf_op jit(solution)/shard_map/ppermute | solution.py:361
  146.1 14.1 %collective-permute-start.5 = (f32[2,256,256]{2,1,0:T(8,128)}, f32[2,256,256]{2,1,0:T(8,128)}, u32[]{:S(2)}, u32[]{:S(2)}) collective-permute-start(f32[2,256,256]{2,1,0:T(8,128)} %slice_add_fusion.2), channel_id=1, source_target_pairs={{0,1},{1,2},{2,3},{3,4},{4,5},{5,6},{6,7},{7,8},{8,9},{9,10},{10,1... | collective-permute-start | bytes 1572872 | tf_op jit(solution)/shard_map/ppermute | solution.py:323
  (5 other events, 10.6 us)

commit v2 on v0

v2 whole, which is shorter than its diff:
```python
import functools
import math

import jax
import jax.numpy as jnp
import numpy as np
from jax import lax
from jax.experimental import pallas as pl
from jax.experimental.pallas import tpu as pltpu
from jax.sharding import PartitionSpec as P

FLOOR_SQUARED = 0.25 * 0.25
OBJECT_RATE = 0.5
PIX = 256
HALF = 128
ROWS = 16
F32 = jnp.float32
BF16 = jnp.bfloat16


TILES = 4


def dft_tables():
    freq = np.arange(HALF)[:, None]
    place = np.arange(HALF)[None, :]
    tables = []
    for odd in (0, 1):
        angle = -2.0 * math.pi * (((2 * freq + odd) * place) % PIX) / PIX
        real, imag = np.cos(angle) / 16.0, np.sin(angle) / 16.0
        whole = np.block([[real, -imag], [imag, real]])
        for matrix in (whole, whole.T):
            high = matrix.astype(jnp.bfloat16)
            tables += [high, (matrix - high.astype(np.float64)).astype(jnp.bfloat16)]
    return np.stack(tables)


def split(value):
    high = value.astype(BF16)
    return high, (value - high.astype(F32)).astype(BF16)


def slot_group(group, lane, window_ref, acc_ref, pacc_ref, probe_ref, measured_ref, table_ref, work):
    patch, probe_r, stack, lanes, spec_e, spec_o = work

    for g in group:
        p, turn = g["p"], g["turn"]
        for i in range(HALF // ROWS):
            pieces = {}
            for half in range(2):
                base = half * HALF + i * ROWS
                planes = []
                for plane in range(2):
                    seen = window_ref[plane, pl.ds(g["tile"], 3), pl.ds(g["top"] + base, ROWS), :]
                    window = (jnp.where(lane < turn, seen[2], seen[0]), seen[1])
                    rolled = [
                        pltpu.roll(probe_ref[plane, base : base + ROWS, t * HALF : (t + 1) * HALF], turn, 1)
                        for t in range(2)
                    ]
                    probe = (
                        jnp.where(lane < turn, rolled[1], rolled[0]),
                        jnp.where(lane < turn, rolled[0], rolled[1]),
                    )
                    for t in range(2):
                        at = (p, plane, slice(base, base + ROWS), slice(t * HALF, (t + 1) * HALF))
                        patch[at] = window[t]
                        probe_r[at] = probe[t]
                    planes.append((window, probe))
                for t in range(2):
                    o_re, q_re = planes[0][0][t], planes[0][1][t]
                    o_im, q_im = planes[1][0][t], planes[1][1][t]
                    pieces[half, t] = (q_re * o_re - q_im * o_im, q_re * o_im + q_im * o_re)
            for t in range(2):
                for c in range(2):
                    upper, under = pieces[0, t][c], pieces[1, t][c]
                    for j, value in enumerate((upper + under, upper - under)):
                        high, low = split(value)
                        r = c * HALF + i * ROWS
                        stack[p, j, r : r + ROWS, t * HALF : (t + 1) * HALF] = low
                        stack[p, j, PIX + r : PIX + r + ROWS, t * HALF : (t + 1) * HALF] = high

    def left_product(p, odd, transposed):
        high = table_ref[4 * odd + 2 * transposed]
        low = table_ref[4 * odd + 2 * transposed + 1]
        both = stack[p, odd]
        return jnp.dot(
            jnp.concatenate([high, high, low], axis=1),
            jnp.concatenate([both, both[PIX:]], axis=0),
            preferred_element_type=F32,
        )

    def right_product(p, odd, transposed):
        high = table_ref[4 * odd + 2 * transposed]
        low = table_ref[4 * odd + 2 * transposed + 1]
        both = lanes[p, odd]
        return jnp.dot(
            jnp.concatenate([both, both[:, PIX:]], axis=1),
            jnp.concatenate([high, high, low], axis=0),
            preferred_element_type=F32,
        )

    for g in group:
        p = g["p"]
        spec_e[p] = left_product(p, 0, 0)
        spec_o[p] = left_product(p, 1, 0)
    for g in group:
        p = g["p"]
        for half, source in enumerate((spec_e, spec_o)):
            for i in range(HALF // ROWS):
                r = half * HALF + i * ROWS
                for c in range(2):
                    s = c * HALF + i * ROWS
                    first = source[p, s : s + ROWS, :HALF]
                    second = source[p, s : s + ROWS, HALF:]
                    for j, value in enumerate((first + second, first - second)):
                        high, low = split(value)
                        lanes[p, j, r : r + ROWS, c * HALF : (c + 1) * HALF] = low
                        lanes[p, j, r : r + ROWS, PIX + c * HALF : PIX + (c + 1) * HALF] = high
    for g in group:
        p = g["p"]
        spec_e[p] = right_product(p, 0, 1)
        spec_o[p] = right_product(p, 1, 1)
    for g in group:
        p = g["p"]
        for j, source in enumerate((spec_e, spec_o)):
            for i in range(PIX // ROWS):
                r = i * ROWS
                re = source[p, r : r + ROWS, :HALF]
                im = source[p, r : r + ROWS, HALF:]
                amplitude = measured_ref[g["index"], r : r + ROWS, j * HALF : (j + 1) * HALF]
                factor = amplitude * lax.rsqrt(jnp.maximum(re * re + im * im, FLOOR_SQUARED))
                for c, value in enumerate((re * factor, im * factor)):
                    high, low = split(value)
                    lanes[p, j, r : r + ROWS, c * HALF : (c + 1) * HALF] = low
                    lanes[p, j, r : r + ROWS, PIX + c * HALF : PIX + (c + 1) * HALF] = high
    for g in group:
        p = g["p"]
        spec_e[p] = right_product(p, 0, 0)
        spec_o[p] = right_product(p, 1, 0)
    for g in group:
        p = g["p"]
        for j in range(2):
            for i in range(HALF // ROWS):
                r = j * HALF + i * ROWS
                for c in range(2):
                    first = spec_e[p, r : r + ROWS, c * HALF : (c + 1) * HALF]
                    second = spec_o[p, r : r + ROWS, c * HALF : (c + 1) * HALF]
                    for t, value in enumerate((first + second, first - second)):
                        high, low = split(value)
                        s = c * HALF + i * ROWS
                        stack[p, j, s : s + ROWS, t * HALF : (t + 1) * HALF] = low
                        stack[p, j, PIX + s : PIX + s + ROWS, t * HALF : (t + 1) * HALF] = high
    for g in group:
        p = g["p"]
        spec_e[p] = left_product(p, 0, 1)
        spec_o[p] = left_product(p, 1, 1)
    for g in group:
        p, turn = g["p"], g["turn"]
        back = (HALF - turn) % HALF
        for i in range(HALF // ROWS):
            for half in range(2):
                base = half * HALF + i * ROWS
                rows = slice(base, base + ROWS)
                object_terms, probe_terms = [], []
                for t in range(2):
                    cols = slice(t * HALF, (t + 1) * HALF)
                    o_re, o_im = patch[p, 0, rows, cols], patch[p, 1, rows, cols]
                    q_re, q_im = probe_r[p, 0, rows, cols], probe_r[p, 1, rows, cols]
                    found = []
                    for c in range(2):
                        s = c * HALF + i * ROWS
                        first = spec_e[p, s : s + ROWS, cols]
                        second = spec_o[p, s : s + ROWS, cols]
                        found.append(first + second if half == 0 else first - second)
                    d_re = jnp.where(g["live"], found[0] - (q_re * o_re - q_im * o_im), 0.0)
                    d_im = jnp.where(g["live"], found[1] - (q_re * o_im + q_im * o_re), 0.0)
                    object_terms.append((q_re * d_re + q_im * d_im, q_re * d_im - q_im * d_re))
                    probe_terms.append((o_re * d_re + o_im * d_im, o_re * d_im - o_im * d_re))
                spots = [
                    (plane, pl.ds(g["tile"], 3), pl.ds(g["top"] + base, ROWS), slice(None)) for plane in range(2)
                ]
                held = [acc_ref[spot] for spot in spots]
                for plane in range(2):
                    mixed, pure = object_terms[0][plane], object_terms[1][plane]
                    acc_ref[spots[plane]] = jnp.stack([
                        held[plane][0] + jnp.where(lane < turn, 0.0, mixed),
                        held[plane][1] + pure,
                        held[plane][2] + jnp.where(lane < turn, mixed, 0.0),
                    ])
                for plane in range(2):
                    rolled = [pltpu.roll(probe_terms[t][plane], back, 1) for t in range(2)]
                    part = slice(i * ROWS, (i + 1) * ROWS)
                    pacc_ref[plane, half, part, :] += jnp.where(lane < HALF - turn, rolled[0], rolled[1])
                    pacc_ref[plane, 2 + half, part, :] += jnp.where(lane < HALF - turn, rolled[1], rolled[0])


def slot_loop(pairs, local, count_ref, top_ref, left_ref, order, refs):
    lane = lax.broadcasted_iota(jnp.int32, (ROWS, HALF), 1)

    def enlist(s, n):
        inside = (top_ref[s] <= PIX) & (left_ref[s] <= PIX)
        mine = inside if local else jnp.logical_not(inside)

        @pl.when(mine)
        def _():
            order[n] = s

        return n + mine.astype(jnp.int32)

    total = lax.fori_loop(jnp.int32(0), count_ref[0], enlist, jnp.int32(0))

    def body(step, carry):
        group = []
        for p in range(pairs):
            place = step * pairs + p
            index = order[jnp.minimum(place, total - 1)]
            left = left_ref[index]
            group.append(dict(
                p=p, index=index, live=place < total, top=top_ref[index], tile=left // HALF, turn=left % HALF,
            ))
        slot_group(group, lane, *refs)
        return carry

    lax.fori_loop(jnp.int32(0), (total + pairs - 1) // pairs, body, jnp.int32(0))


def order_kernel(count_ref, measured_ref, ordered_out, raw, sems):
    copies = [
        pltpu.make_async_copy(measured_ref.at[:, :, pl.ds(t * HALF, HALF)], raw.at[t], sems.at[t])
        for t in range(2)
    ]
    for copy in copies:
        copy.start()
    lane = lax.broadcasted_iota(jnp.int32, (HALF, HALF), 1)
    first = lane < 64
    even_first = jnp.where(first, 2 * lane, 2 * lane - 127)
    odd_first = jnp.where(first, 2 * lane + 1, 2 * lane - 128)
    for copy in copies:
        copy.wait()

    def reorder(s, carry):
        for parity in range(2):
            rows = pl.ds(parity, HALF, stride=2)
            left = jnp.take_along_axis(raw[0, s, rows, :], even_first, axis=1)
            right = jnp.take_along_axis(raw[1, s, rows, :], odd_first, axis=1)
            out = slice(parity * HALF, (parity + 1) * HALF)
            ordered_out[s, out, :HALF] = jnp.where(first, left, right)
            ordered_out[s, out, HALF:] = pltpu.roll(jnp.where(first, right, left), 64, 1)
        return carry

    lax.fori_loop(jnp.int32(0), count_ref[0], reorder, jnp.int32(0))


def local_kernel(
    pairs,
    count_ref, top_ref, left_ref, object_ref, ordered_ref, probe_ref, table_ref,
    acc_out, pacc_out,
    ext, order, sems, *work,
):
    copies = [
        pltpu.make_async_copy(object_ref.at[:, :, pl.ds(t * HALF, HALF)], ext.at[:, t], sems.at[t])
        for t in range(TILES)
    ]
    for copy in copies:
        copy.start()
    acc_out[...] = jnp.zeros_like(acc_out)
    pacc_out[...] = jnp.zeros_like(pacc_out)
    for copy in copies:
        copy.wait()
    slot_loop(
        pairs, True, count_ref, top_ref, left_ref, order,
        (ext, acc_out, pacc_out, probe_ref, ordered_ref, table_ref, work),
    )


def rest_kernel(
    pairs,
    count_ref, top_ref, left_ref, place_ref, object_ref, top_rim, bottom_rim, lower_rim, corner_rim, held_ref,
    pacc_ref, ordered_ref, probe_ref, table_ref,
    tile_out, top_out, bottom_out, lower_out, mine_out, other_out,
    ext, acc, pacc, order, sems, *work,
):
    copies = []

    def bring(source, target):
        copies.append(pltpu.make_async_copy(source, target, sems.at[len(copies)]))
        copies[-1].start()

    for t in range(TILES):
        cols = pl.ds(t * HALF, HALF)
        bring(object_ref.at[:, :, cols], ext.at[:, t, pl.ds(0, 512)])
        bring(lower_rim.at[:, :, cols], ext.at[:, t, pl.ds(512, PIX)])
        bring(held_ref.at[:, t], acc.at[:, t, pl.ds(0, 512)])
    for t in range(2):
        cols = pl.ds(t * HALF, HALF)
        bring(top_rim.at[:, :, cols], ext.at[:, TILES + t, pl.ds(0, PIX)])
        bring(bottom_rim.at[:, :, cols], ext.at[:, TILES + t, pl.ds(PIX, PIX)])
        bring(corner_rim.at[:, :, cols], ext.at[:, TILES + t, pl.ds(512, PIX)])
    acc[:, 0:TILES, 512:768, :] = jnp.zeros((2, TILES, PIX, HALF), F32)
    acc[:, TILES:, :, :] = jnp.zeros((2, 2, 768, HALF), F32)
    pacc[...] = pacc_ref[...]
    for copy in copies:
        copy.wait()
    slot_loop(
        pairs, False, count_ref, top_ref, left_ref, order,
        (ext, acc, pacc, probe_ref, ordered_ref, table_ref, work),
    )
    y_pos, core = place_ref[0], place_ref[1]
    for k in range(4):
        mine_out[k] = pacc[core, (y_pos + k) % 4]
        other_out[k] = pacc[1 - core, (y_pos + k) % 4]
    for t in range(TILES):
        cols = slice(t * HALF, (t + 1) * HALF)
        tile_out[:, :, cols] = ext[:, t, 0:512, :] + OBJECT_RATE * acc[:, t, 0:512, :]
    for t in range(TILES + 2):
        lower_out[:, :, t * HALF : (t + 1) * HALF] = OBJECT_RATE * acc[:, t, 512:768, :]
    for t in range(2):
        cols = slice(t * HALF, (t + 1) * HALF)
        top_out[:, :, cols] = OBJECT_RATE * acc[:, TILES + t, 0:PIX, :]
        bottom_out[:, :, cols] = OBJECT_RATE * acc[:, TILES + t, PIX:512, :]


VMEM = pl.BlockSpec(memory_space=pltpu.VMEM)
SMEM = pl.BlockSpec(memory_space=pltpu.SMEM)
ANYWHERE = pl.BlockSpec(memory_space=pl.ANY)


def work_shapes(pairs):
    return [
        pltpu.VMEM((pairs, 2, PIX, PIX), F32),
        pltpu.VMEM((pairs, 2, PIX, PIX), F32),
        pltpu.VMEM((pairs, 2, 2 * PIX, PIX), BF16),
        pltpu.VMEM((pairs, 2, PIX, 2 * PIX), BF16),
        pltpu.VMEM((pairs, PIX, PIX), F32),
        pltpu.VMEM((pairs, PIX, PIX), F32),
    ]


QUARTER = jax.ShapeDtypeStruct((HALF, HALF), F32)
QUARTERS = jax.ShapeDtypeStruct((4, HALF, HALF), F32)
WHOLE_TILE = jax.ShapeDtypeStruct((2, 512, 512), F32)
LOWER = jax.ShapeDtypeStruct((2, PIX, 768), F32)
TOKEN = jax.ShapeDtypeStruct((8, HALF), F32)
BLOCK = jax.ShapeDtypeStruct((2, PIX, PIX), F32)


def in_order(count, measured):
    return pl.pallas_call(
        order_kernel,
        in_specs=[SMEM, ANYWHERE],
        out_specs=VMEM,
        out_shape=jax.ShapeDtypeStruct((16, PIX, PIX), F32),
        scratch_shapes=[pltpu.VMEM((2, 16, PIX, HALF), F32), pltpu.SemaphoreType.DMA((2,))],
        compiler_params=pltpu.CompilerParams(vmem_limit_bytes=10 * 1024 * 1024),
        cost_estimate=pl.CostEstimate(flops=0, bytes_accessed=16 * 2**20, transcendentals=0),
        name="order_measured",
    )(count, measured)


def process_local(count, tops, lefts, tile, ordered, probe, tables):
    pairs = 2
    return pl.pallas_call(
        functools.partial(local_kernel, pairs),
        in_specs=[SMEM] * 3 + [ANYWHERE] + [VMEM] * 3,
        out_specs=[VMEM] * 2,
        out_shape=[jax.ShapeDtypeStruct((2, TILES + 1, 512, HALF), F32), jax.ShapeDtypeStruct((2, 4, HALF, HALF), F32)],
        scratch_shapes=[
            pltpu.VMEM((2, TILES + 1, 512, HALF), F32),
            pltpu.SMEM((16,), jnp.int32),
            pltpu.SemaphoreType.DMA((TILES,)),
        ] + work_shapes(pairs),
        compiler_params=pltpu.CompilerParams(vmem_limit_bytes=22 * 1024 * 1024),
        cost_estimate=pl.CostEstimate(flops=6 * 10**9, bytes_accessed=20 * 2**20, transcendentals=2**20),
        name="local_slots",
    )(count, tops, lefts, tile, ordered, probe, tables)


def process_rest(count, tops, lefts, place, tile, top, bottom, lower, corner, held, pacc, ordered, probe, tables):
    pairs = 2
    return pl.pallas_call(
        functools.partial(rest_kernel, pairs),
        in_specs=[SMEM] * 4 + [ANYWHERE] * 6 + [VMEM] * 4,
        out_specs=[VMEM] * 6,
        out_shape=[WHOLE_TILE] + [BLOCK] * 2 + [LOWER] + [QUARTERS] * 2,
        scratch_shapes=[
            pltpu.VMEM((2, TILES + 2, 768, HALF), F32),
            pltpu.VMEM((2, TILES + 2, 768, HALF), F32),
            pltpu.VMEM((2, 4, HALF, HALF), F32),
            pltpu.SMEM((16,), jnp.int32),
            pltpu.SemaphoreType.DMA((18,)),
        ] + work_shapes(pairs),
        compiler_params=pltpu.CompilerParams(vmem_limit_bytes=30 * 1024 * 1024),
        cost_estimate=pl.CostEstimate(flops=13 * 10**9, bytes_accessed=20 * 2**20, transcendentals=2**20),
        name="other_slots",
    )(count, tops, lefts, place, tile, top, bottom, lower, corner, held, pacc, ordered, probe, tables)


def joined(kernel, name, operands, outs, smem=0, beside=()):
    return pl.pallas_call(
        kernel,
        in_specs=[SMEM] * smem + [VMEM] * (len(operands) - smem) + [ANYWHERE] * len(beside),
        out_specs=[VMEM] * len(outs),
        out_shape=list(outs),
        compiler_params=pltpu.CompilerParams(vmem_limit_bytes=16 * 1024 * 1024),
        cost_estimate=pl.CostEstimate(flops=2**18, bytes_accessed=2**20, transcendentals=0),
        name=name,
    )(*operands, *beside)


def pair_kernel(mine_ref, came_ref, *outs):
    for k, out in enumerate(outs):
        out[...] = mine_ref[k] + came_ref[k]


def ring_kernel(own, one, two, three, *rest):
    rest[-1][...] = (own[...] + two[...]) + (one[...] + three[...])


def corner_kernel(own, one, two, three, top, lower, bottom, part, rim):
    ring_kernel(own, one, two, three, part)
    rim[...] = top[...] + lower[:, :, 512:]


def tile_kernel(tile, top, bottom, lower, out, token):
    out[:, :PIX, :PIX] = tile[:, :PIX, :PIX] + (lower[:, :, :PIX] + top[...])
    out[:, :PIX, PIX:] = tile[:, :PIX, PIX:] + lower[:, :, PIX:512]
    out[:, PIX:, :PIX] = tile[:, PIX:, :PIX] + bottom[...]
    out[:, PIX:, PIX:] = tile[:, PIX:, PIX:]
    token[...] = jnp.zeros_like(token)


def half_kernel(place_ref, own, one, two, three, token, half):
    for k, part in enumerate((own, one, two, three)):
        half[(place_ref[0] + 4 - k) % 4] = part[...]


def probe_kernel(place_ref, root_ref, probe, half, other, out):
    core, root = place_ref[1], root_ref[0]
    for q in range(4):
        at = (slice(q % 2 * HALF, (q % 2 + 1) * HALF), slice(q // 2 * HALF, (q // 2 + 1) * HALF))
        mine, theirs = half[q], other[q]
        out[(0,) + at] = probe[(0,) + at] + jnp.where(core == 0, mine, theirs) / root
        out[(1,) + at] = probe[(1,) + at] + jnp.where(core == 0, theirs, mine) / root


def passed_along(shard, axis, by):
    peers = lax.axis_size(axis)
    pairs = [(i, i + by) for i in range(peers) if 0 <= i + by < peers]
    return lax.ppermute(shard, axis, pairs)


def over_core(v):
    return lax.ppermute(v, "row", [(i, i ^ 1) for i in range(8)])


def over_x(v, k):
    return lax.ppermute(v, "row", [(i, (i + 2 * k) % 8) for i in range(8)])


def over_y(v, k):
    return lax.ppermute(v, "col", [(i, (i + 4 * k) % 16) for i in range(16)])


def over_z(v, k):
    return lax.ppermute(v, "col", [(i, i // 4 * 4 + (i % 4 + k) % 4) for i in range(16)])


def per_device(object_field, probe_field, measured, positions, counts):
    row_pos = lax.axis_index("row")
    col_pos = lax.axis_index("col")
    own_device = row_pos * lax.axis_size("col") + col_pos
    place = jnp.stack([col_pos // 4, row_pos % 2])
    root = jnp.sqrt(jnp.sum(counts).astype(F32))[None]
    tables = jnp.asarray(dft_tables())
    top = passed_along(object_field[:, :PIX, :PIX], "col", -1)
    bottom = passed_along(object_field[:, PIX:, :PIX], "col", -1)
    lower = passed_along(object_field[:, :PIX, :], "row", -1)
    corner = passed_along(top, "row", -1)
    count = counts[own_device][None]
    where = (count, positions[:, 0] - row_pos * 512, positions[:, 1] - col_pos * 512)
    ordered = in_order(count, measured)
    held, pacc = process_local(*where, object_field, ordered, probe_field, tables)
    tile, top_sum, bottom_sum, lower_sum, mine, other = process_rest(
        *where, place, object_field, top, bottom, lower, corner, held, pacc, ordered, probe_field, tables
    )
    lower_back = passed_along(lower_sum, "row", 1)
    bottom_back = passed_along(bottom_sum, "col", 1)
    quarters = joined(pair_kernel, "pair_sum", (mine, over_core(other)), [QUARTER] * 4)
    (part,) = joined(
        ring_kernel, "y_sum", [quarters[0]] + [over_y(quarters[k], k) for k in (1, 2, 3)], [QUARTER], beside=[root]
    )
    part, rim = joined(
        corner_kernel, "z_sum", [part] + [over_z(part, k) for k in (1, 2, 3)] + [top_sum, lower_back],
        [QUARTER, BLOCK], beside=[bottom_back],
    )
    top_back = passed_along(rim, "col", 1)
    (part,) = joined(ring_kernel, "x_sum", [part] + [over_x(part, k) for k in (1, 2, 3)], [QUARTER])
    new_object, token = joined(
        tile_kernel, "new_tile", (tile, top_back, bottom_back, lower_back), [WHOLE_TILE, TOKEN]
    )
    (half,) = joined(
        half_kernel, "half", [place, part] + [over_y(part, k) for k in (1, 2, 3)], [QUARTERS], smem=1,
        beside=[token],
    )
    (new_probe,) = joined(
        probe_kernel, "new_probe", (place, root, probe_field, half, over_core(half)), [BLOCK], smem=2,
    )
    return (new_object, new_probe)


def solution(mesh):
    placed = (
        P(None, "row", "col"),
        P(),
        P(("row", "col"), None, None),
        P(("row", "col"), None),
        P(),
    )
    return jax.shard_map(
        per_device,
        mesh=mesh,
        in_specs=placed,
        out_specs=(P(None, "row", "col"), P()),
        check_vma=False,
    )
```

time: 943 us -> 114 us (0.12)
  starting transfers between devices: 597 us -> 47.1 us
  waiting for transfers between devices: 219 us -> 15 us
  matrix products: 51.7 us -> 0 us
  Pallas kernels: 0 us -> 39.2 us
  other arithmetic: 19.5 us -> 0.78 us
  local copies, waits for them, and re-layouts: 25.9 us -> 8.67 us
  between operations: 14.9 us -> 1.62 us
  loops' own time: 9.73 us -> 0 us
    ppermute x4 -> x7, starting transfers between devices: 597 us -> 14.4 us  [passed_along(): return lax.ppermute(shard, axis, pairs)]
    psum x1 -> x0, waiting for transfers between devices: 162 us -> none  [per_device(): probe_total = lax.psum(probe_sum, ('row', 'col'))]
    ppermute x4 -> x7, waiting for transfers between devices: 56.5 us -> 1.83 us  [passed_along(): return lax.ppermute(shard, axis, pairs)]
    dot_general x32 -> x0, matrix products: 51.7 us -> none  [matmul(): jnp.dot(left_side, right_side, precision=lax.Precision.HIGHEST, preferred...]
    pallas_call x0 -> x10, Pallas kernels: none -> 39.2 us  [the longest x1 21.8 us: process_rest(): pl.pallas_call(functools.partial(rest_kernel, pairs), in_specs=[SMEM] * 4...]
    ppermute x0 -> x14, starting transfers between devices: none -> 32.7 us  [the longest x6 15.6 us: over_y(): return lax.ppermute(v, 'col', [(i, (i + 4 * k) % 16) for i in range(16)])]
    dynamic_update_slice x2 -> x0, local copies, waits for them, and re-layouts: 13.6 us -> none  [add_window(): lax.dynamic_update_slice(target, current + object_term, (zero_index, top_...]
    add x8 -> x0, other arithmetic: 13.2 us -> none  [the longest x2 3.01 us: add_window(): current + object_term]
  transfers between devices with their start and end apart: 5 -> 21, of which waited for: 4 -> 11; matrix products, arithmetic and copies ran while one was open for 0% -> 2% of each run, Pallas kernels for 0% -> 14%
where the time goes in v2:
time: 114 us; the launch traced here: 112 us
  starting transfers between devices  47.1 us (41%)
  Pallas kernels  39.2 us (34%)
  waiting for transfers between devices  15 us (13%)
  local copies, waits for them, and re-layouts  8.67 us (8%)
  between operations  1.62 us (1%)
    pallas_call x1, Pallas kernels, process_rest(): pl.pallas_call(functools.partial(rest_kernel, pairs), in_specs=[SMEM] * 4...  21.8 us
    ppermute x6, starting transfers between devices, over_y(): return lax.ppermute(v, 'col', [(i, (i + 4 * k) % 16) for i in range(16)])  15.6 us
    ppermute x7, starting transfers between devices, passed_along(): return lax.ppermute(shard, axis, pairs)  14.4 us
    ppermute x3, starting transfers between devices, over_z(): lax.ppermute(v, 'col', [(i, i // 4 * 4 + (i % 4 + k) % 4) for i in range(...  8.46 us
    pallas_call x1, Pallas kernels, process_local(): pl.pallas_call(functools.partial(local_kernel, pairs), in_specs=[SMEM] *...  7.7 us
    ppermute x2, starting transfers between devices, over_core(): return lax.ppermute(v, 'row', [(i, i ^ 1) for i in range(8)])  5.91 us
    pallas_call x1, Pallas kernels, in_order(): pl.pallas_call(order_kernel, in_specs=[SMEM, ANYWHERE], out_specs=VMEM, o...  5.38 us
    ppermute x3, waiting for transfers between devices, over_z(): lax.ppermute(v, 'col', [(i, i // 4 * 4 + (i % 4 + k) % 4) for i in range(...  5.08 us
  transfers between devices with their start and end apart: 21, of which 11 were waited for; matrix products, arithmetic and copies ran while one was open for 2% of the time, Pallas kernels for 14%

profile of v2, /device:TPU:1, one launch (start us, length us, event | category | flops | bytes accessed | tf_op | source)
XLA Modules:
  0.0 112.4 jit_solution(4016571471237689824)
XLA Ops:
  0.6 2.4 %fusion = (f32[2,256,256]{2,1,0:T(8,128)}, f32[2,256,256]{2,1,0:T(8,128)}) fusion(f32[2,512,512]{2,1,0:T(8,128)} %object_ref.3), kind=kLoop, calls=%fused_computation.3 | loop fusion | bytes 2097152 | tf_op jit(solution)/shard_map/slice | solution.py:476
  5.4 3.3 %collective-permute-start.2 = (f32[2,256,512]{2,1,0:T(8,128)}, f32[2,256,512]{2,1,0:T(8,128)}, u32[]{:S(2)}, u32[]{:S(2)}) collective-permute-start(f32[2,256,512]{2,1,0:T(8,128)} %slice.19), channel_id=1, source_target_pairs={{16,0},{32,16},{48,32},{64,48},{80,64},{96,80},{112,96},{17,1},{33... | collective-permute-start | bytes 3145736 | tf_op jit(solution)/shard_map/ppermute | solution.py:449
  10.7 2.2 %copy-done = f32[16,256,256]{2,1,0:T(8,128)S(1)} copy-done((f32[16,256,256]{2,1,0:T(8,128)S(1)}, f32[16,256,256]{2,1,0:T(8,128)}, u32[]{:S(2)}) %copy-start) | copy-done | bytes 4194328
  12.9 5.4 %order_measured.1.ordered_ref = f32[16,256,256]{2,1,0:T(8,128)S(1)} custom-call(s32[1]{0:T(128)} %dynamic_slice.3.count_ref, f32[16,256,256]{2,1,0:T(8,128)S(1)} %copy-done), custom_call_target="tpu_custom_call" | custom-call | bytes 16777216 | tf_op jit(solution)/shard_map/order_measured/pallas_call | solution.py:348
  19.3 4.0 %collective-permute-start.3 = (f32[2,256,256]{2,1,0:T(8,128)S(1)}, f32[2,256,256]{2,1,0:T(8,128)S(1)}, u32[]{:S(2)}, u32[]{:S(2)}) collective-permute-start(f32[2,256,256]{2,1,0:T(8,128)S(1)} %collective-permute-done.top_rim), channel_id=1, source_target_pairs={{16,0},{32,16},{48,32},{64,48},{80,64},{96,80},{112,96},{17,1},{33... | collective-permute-start | bytes 1572872 | tf_op jit(solution)/shard_map/ppermute | solution.py:449
  23.3 7.7 %local_slots.1 = (f32[2,5,512,128]{3,2,1,0:T(8,128)S(1)}, f32[2,4,128,128]{3,2,1,0:T(8,128)S(1)}) custom-call(s32[1]{0:T(128)} %dynamic_slice.3.count_ref, s32[16]{0:T(128)S(1)} %get-tuple-element.37.top_ref, s32[16]{0:T(128)S(1)} %get-tuple-element.36.left_ref, f32[2,512,512]{2,1,0:T(8,128)S(1)} %copy-done.1, ...), custom_call_target="tpu_custom_call" | custom-call | flops 6000000000 | bytes 20971520 | tf_op jit(solution)/shard_map/local_slots/pallas_call | solution.py:362
  32.5 21.8 %other_slots.1 = (f32[2,512,512]{2,1,0:T(8,128)S(1)}, f32[2,256,256]{2,1,0:T(8,128)S(1)}, f32[2,256,256]{2,1,0:T(8,128)}, f32[2,256,768]{2,1,0:T(8,128)}, f32[4,...) custom-call(s32[1]{0:T(128)} %dynamic_slice.3.count_ref, s32[16]{0:T(128)S(1)} %get-tuple-element.37.top_ref, ...), custom_call_target="tpu_custom_call" | custom-call | flops 12999999488 | bytes 20971520 | tf_op jit(solution)/shard_map/other_slots/pallas_call | solution.py:380
  54.3 1.3 %copy-done.2 = f32[2,512,512]{2,1,0:T(8,128)} copy-done((f32[2,512,512]{2,1,0:T(8,128)}, f32[2,512,512]{2,1,0:T(8,128)S(1)}, u32[]{:S(2)}) %copy-start.2) | copy-done | bytes 2097176
  55.6 1.9 %collective-permute-start.11 = (f32[2,256,768]{2,1,0:T(8,128)}, f32[2,256,768]{2,1,0:T(8,128)S(1)}, u32[]{:S(2)}, u32[]{:S(2)}) collective-permute-start(f32[2,256,768]{2,1,0:T(8,128)} %get-tuple-element.28), channel_id=1, source_target_pairs={{0,16},{16,32},{32,48},{48,64},{64,80},{80,96},{96,112},{1,17},{17... | collective-permute-start | bytes 4718600 | tf_op jit(solution)/shard_map/ppermute | solution.py:449
  57.5 1.3 %collective-permute-start.12 = (f32[2,256,256]{2,1,0:T(8,128)}, f32[2,256,256]{2,1,0:T(8,128)S(1)}, u32[]{:S(2)}, u32[]{:S(2)}) collective-permute-start(f32[2,256,256]{2,1,0:T(8,128)} %get-tuple-element.29), channel_id=1, source_target_pairs={{0,1},{1,2},{2,3},{3,4},{4,5},{5,6},{6,7},{7,8},{8,9},{9,10},{10,1... | collective-permute-start | bytes 1572872 | tf_op jit(solution)/shard_map/ppermute | solution.py:449
  59.5 1.7 %collective-permute-done.4.came_ref = f32[4,128,128]{2,1,0:T(8,128)S(1)} collective-permute-done((f32[4,128,128]{2,1,0:T(8,128)S(1)}, f32[4,128,128]{2,1,0:T(8,128)S(1)}, u32[]{:S(2)}, u32[]{:S(2)}) %collective-permute-start.4) | collective-permute-done | bytes 262176 | tf_op jit(solution)/shard_map/ppermute | solution.py:453
  61.9 5.8 %collective-permute-start.5 = (f32[128,128]{1,0:T(8,128)}, f32[128,128]{1,0:T(8,128)S(1)}, u32[]{:S(2)}, u32[]{:S(2)}) collective-permute-start(f32[128,128]{1,0:T(8,128)} %get-tuple-element.24), channel_id=1, source_target_pairs={{0,4},{1,5},{2,6},{3,7},{4,8},{5,9},{6,10},{7,11},{8,12},{9,13},{1... | collective-permute-start | bytes 196616 | tf_op jit(solution)/shard_map/ppermute | solution.py:461
  67.7 5.9 %collective-permute-start.6 = (f32[128,128]{1,0:T(8,128)S(1)}, f32[128,128]{1,0:T(8,128)S(1)}, u32[]{:S(2)}, u32[]{:S(2)}) collective-permute-start(f32[128,128]{1,0:T(8,128)S(1)} %get-tuple-element.25), channel_id=1, source_target_pairs={{0,8},{1,9},{2,10},{3,11},{4,12},{5,13},{6,14},{7,15},{8,0},{9,1},... | collective-permute-start | bytes 196616 | tf_op jit(solution)/shard_map/ppermute | solution.py:461
  75.0 1.7 %collective-permute-done.6.two = f32[128,128]{1,0:T(8,128)S(1)} collective-permute-done((f32[128,128]{1,0:T(8,128)S(1)}, f32[128,128]{1,0:T(8,128)S(1)}, u32[]{:S(2)}, u32[]{:S(2)}) %collective-permute-start.6) | collective-permute-done | bytes 65568 | tf_op jit(solution)/shard_map/ppermute | solution.py:461
  77.0 7.2 %collective-permute-start.10 = (f32[128,128]{1,0:T(8,128)S(1)}, f32[128,128]{1,0:T(8,128)S(1)}, u32[]{:S(2)}, u32[]{:S(2)}) collective-permute-start(f32[128,128]{1,0:T(8,128)S(1)} %y_sum.1.own), channel_id=1, source_target_pairs={{0,3},{1,0},{2,1},{3,2},{4,7},{5,4},{6,5},{7,6},{8,11},{9,8},{10,9... | collective-permute-start | bytes 196616 | tf_op jit(solution)/shard_map/ppermute | solution.py:465
  85.5 5.0 %collective-permute-done.8.one = f32[128,128]{1,0:T(8,128)S(1)} collective-permute-done((f32[128,128]{1,0:T(8,128)S(1)}, f32[128,128]{1,0:T(8,128)S(1)}, u32[]{:S(2)}, u32[]{:S(2)}) %collective-permute-start.8) | collective-permute-done | bytes 65568 | tf_op jit(solution)/shard_map/ppermute | solution.py:465
  90.6 1.3 %collective-permute-start.13 = (f32[2,256,256]{2,1,0:T(8,128)S(1)}, f32[2,256,256]{2,1,0:T(8,128)S(1)}, u32[]{:S(2)}, u32[]{:S(2)}) collective-permute-start(f32[2,256,256]{2,1,0:T(8,128)S(1)} %get-tuple-element.30), channel_id=1, source_target_pairs={{0,1},{1,2},{2,3},{3,4},{4,5},{5,6},{6,7},{7,8},{8,9},{9,10},{10,1... | collective-permute-start | bytes 1572872 | tf_op jit(solution)/shard_map/ppermute | solution.py:449
  92.1 2.6 %collective-permute-start.16 = (f32[128,128]{1,0:T(8,128)S(1)}, f32[128,128]{1,0:T(8,128)S(1)}, u32[]{:S(2)}, u32[]{:S(2)}) collective-permute-start(f32[128,128]{1,0:T(8,128)S(1)} %get-tuple-element.32.own), channel_id=1, source_target_pairs={{0,96},{16,112},{32,0},{48,16},{64,32},{80,48},{96,64},{112,80},{1... | collective-permute-start | bytes 196616 | tf_op jit(solution)/shard_map/ppermute | solution.py:457
  94.7 2.3 %collective-permute-done.14.one = f32[128,128]{1,0:T(8,128)S(1)} collective-permute-done((f32[128,128]{1,0:T(8,128)S(1)}, f32[128,128]{1,0:T(8,128)S(1)}, u32[]{:S(2)}, u32[]{:S(2)}) %collective-permute-start.14) | collective-permute-done | bytes 65568 | tf_op jit(solution)/shard_map/ppermute | solution.py:457
  98.0 1.8 %collective-permute-start.18 = (f32[128,128]{1,0:T(8,128)S(1)}, f32[128,128]{1,0:T(8,128)S(1)}, u32[]{:S(2)}, u32[]{:S(2)}) collective-permute-start(f32[128,128]{1,0:T(8,128)S(1)} %x_sum.1.own), channel_id=1, source_target_pairs={{0,8},{1,9},{2,10},{3,11},{4,12},{5,13},{6,14},{7,15},{8,0},{9,1},... | collective-permute-start | bytes 196616 | tf_op jit(solution)/shard_map/ppermute | solution.py:461
  99.9 2.0 %collective-permute-start.19 = (f32[128,128]{1,0:T(8,128)S(1)}, f32[128,128]{1,0:T(8,128)S(1)}, u32[]{:S(2)}, u32[]{:S(2)}) collective-permute-start(f32[128,128]{1,0:T(8,128)S(1)} %x_sum.1.own), channel_id=1, source_target_pairs={{0,12},{1,13},{2,14},{3,15},{4,0},{5,1},{6,2},{7,3},{8,4},{9,5},{1... | collective-permute-start | bytes 196616 | tf_op jit(solution)/shard_map/ppermute | solution.py:461
  102.4 1.6 %new_tile.1 = (f32[2,512,512]{2,1,0:T(8,128)}, f32[8,128]{1,0:T(8,128)S(1)}) custom-call(f32[2,512,512]{2,1,0:T(8,128)S(1)} %copy-done.3, f32[2,256,256]{2,1,0:T(8,128)S(1)} %collective-permute-done.13.top, f32[2,256,256]{2,1,0:T(8,128)S(1)} %collective-permute-done.12.bottom, f32[2,256,768]{2,1,0:T(8,128)S(1)} %collective-permute-done.11.lower), custom_call_target="tpu_custom_call" | custom-call | flops 262144 | bytes 1048576 | tf_op jit(solution)/shard_map/new_tile/pallas_call | solution.py:399
  104.5 5.2 %collective-permute-start.20 = (f32[4,128,128]{2,1,0:T(8,128)S(1)}, f32[4,128,128]{2,1,0:T(8,128)S(1)}, u32[]{:S(2)}, u32[]{:S(2)}) collective-permute-start(f32[4,128,128]{2,1,0:T(8,128)S(1)} %half.1), channel_id=1, source_target_pairs={{0,16},{16,0},{32,48},{48,32},{64,80},{80,64},{96,112},{112,96},{1... | collective-permute-start | bytes 786440 | tf_op jit(solution)/shard_map/ppermute | solution.py:453
  110.9 1.4 %new_probe.1 = f32[2,256,256]{2,1,0:T(8,128)} custom-call(s32[2]{0:T(128)S(1)} %pad_add_fusion.place_ref, f32[1]{0:T(128)} %bitcast.4.rest_0_.root_ref, f32[2,256,256]{2,1,0:T(8,128)S(1)} %copy-done.4, f32[4,128,128]{2,1,0:T(8,128)S(1)} %half.1, f32[4,128,128]{2,1,0:T(8,128)S(1)} %collective-permute-done.20.other), custom_call_target="tpu_custom_call" | custom-call | flops 262144 | bytes 1048576 | tf_op jit(solution)/shard_map/new_probe/pallas_call | solution.py:399
  (54 shorter events, 13.8 us)
Async XLA Ops:
  3.1 16.2 %collective-permute-start = (f32[2,256,256]{2,1,0:T(8,128)}, f32[2,256,256]{2,1,0:T(8,128)S(1)}, u32[]{:S(2)}, u32[]{:S(2)}) collective-permute-start(f32[2,256,256]{2,1,0:T(8,128)} %get-tuple-element.35), channel_id=1, source_target_pairs={{1,0},{2,1},{3,2},{4,3},{5,4},{6,5},{7,6},{8,7},{9,8},{10,9},{11,1... | collective-permute-start | bytes 1572872 | tf_op jit(solution)/shard_map/ppermute | solution.py:449
  5.4 26.1 %collective-permute-start.2 = (f32[2,256,512]{2,1,0:T(8,128)}, f32[2,256,512]{2,1,0:T(8,128)}, u32[]{:S(2)}, u32[]{:S(2)}) collective-permute-start(f32[2,256,512]{2,1,0:T(8,128)} %slice.19), channel_id=1, source_target_pairs={{16,0},{32,16},{48,32},{64,48},{80,64},{96,80},{112,96},{17,1},{33... | collective-permute-start | bytes 3145736 | tf_op jit(solution)/shard_map/ppermute | solution.py:449
  8.7 22.3 %collective-permute-start.1 = (f32[2,256,256]{2,1,0:T(8,128)}, f32[2,256,256]{2,1,0:T(8,128)}, u32[]{:S(2)}, u32[]{:S(2)}) collective-permute-start(f32[2,256,256]{2,1,0:T(8,128)} %get-tuple-element.34), channel_id=1, source_target_pairs={{1,0},{2,1},{3,2},{4,3},{5,4},{6,5},{7,6},{8,7},{9,8},{10,9},{11,1... | collective-permute-start | bytes 1572872 | tf_op jit(solution)/shard_map/ppermute | solution.py:449
  12.9 10.4 %copy-start.7 = (bf16[8,256,256]{2,1,0:T(8,128)(2,1)S(1)}, bf16[8,256,256]{2,1,0:T(8,128)(2,1)}, u32[]{:S(2)}) copy-start(bf16[8,256,256]{2,1,0:T(8,128)(2,1)} %constant.44.clone.table_ref) | copy-start | bytes 3145732
  19.3 11.7 %copy-start.5 = (f32[2,256,256]{2,1,0:T(8,128)}, f32[2,256,256]{2,1,0:T(8,128)S(1)}, u32[]{:S(2)}) copy-start(f32[2,256,256]{2,1,0:T(8,128)S(1)} %collective-permute-done.top_rim) | copy-start | bytes 1572868
  19.3 12.2 %collective-permute-start.3 = (f32[2,256,256]{2,1,0:T(8,128)S(1)}, f32[2,256,256]{2,1,0:T(8,128)S(1)}, u32[]{:S(2)}, u32[]{:S(2)}) collective-permute-start(f32[2,256,256]{2,1,0:T(8,128)S(1)} %collective-permute-done.top_rim), channel_id=1, source_target_pairs={{16,0},{32,16},{48,32},{64,48},{80,64},{96,80},{112,96},{17,1},{33... | collective-permute-start | bytes 1572872 | tf_op jit(solution)/shard_map/ppermute | solution.py:449
  55.6 35.0 %collective-permute-start.11 = (f32[2,256,768]{2,1,0:T(8,128)}, f32[2,256,768]{2,1,0:T(8,128)S(1)}, u32[]{:S(2)}, u32[]{:S(2)}) collective-permute-start(f32[2,256,768]{2,1,0:T(8,128)} %get-tuple-element.28), channel_id=1, source_target_pairs={{0,16},{16,32},{32,48},{48,64},{64,80},{80,96},{96,112},{1,17},{17... | collective-permute-start | bytes 4718600 | tf_op jit(solution)/shard_map/ppermute | solution.py:449
  57.5 33.1 %collective-permute-start.12 = (f32[2,256,256]{2,1,0:T(8,128)}, f32[2,256,256]{2,1,0:T(8,128)S(1)}, u32[]{:S(2)}, u32[]{:S(2)}) collective-permute-start(f32[2,256,256]{2,1,0:T(8,128)} %get-tuple-element.29), channel_id=1, source_target_pairs={{0,1},{1,2},{2,3},{3,4},{4,5},{5,6},{6,7},{7,8},{8,9},{9,10},{10,1... | collective-permute-start | bytes 1572872 | tf_op jit(solution)/shard_map/ppermute | solution.py:449
  58.8 2.4 %collective-permute-start.4 = (f32[4,128,128]{2,1,0:T(8,128)S(1)}, f32[4,128,128]{2,1,0:T(8,128)S(1)}, u32[]{:S(2)}, u32[]{:S(2)}) collective-permute-start(f32[4,128,128]{2,1,0:T(8,128)S(1)} %get-tuple-element.22), channel_id=1, source_target_pairs={{0,16},{16,0},{32,48},{48,32},{64,80},{80,64},{96,112},{112,96},{1... | collective-permute-start | bytes 786440 | tf_op jit(solution)/shard_map/ppermute | solution.py:453
  61.9 13.1 %collective-permute-start.5 = (f32[128,128]{1,0:T(8,128)}, f32[128,128]{1,0:T(8,128)S(1)}, u32[]{:S(2)}, u32[]{:S(2)}) collective-permute-start(f32[128,128]{1,0:T(8,128)} %get-tuple-element.24), channel_id=1, source_target_pairs={{0,4},{1,5},{2,6},{3,7},{4,8},{5,9},{6,10},{7,11},{8,12},{9,13},{1... | collective-permute-start | bytes 196616 | tf_op jit(solution)/shard_map/ppermute | solution.py:461
  67.7 9.0 %collective-permute-start.6 = (f32[128,128]{1,0:T(8,128)S(1)}, f32[128,128]{1,0:T(8,128)S(1)}, u32[]{:S(2)}, u32[]{:S(2)}) collective-permute-start(f32[128,128]{1,0:T(8,128)S(1)} %get-tuple-element.25), channel_id=1, source_target_pairs={{0,8},{1,9},{2,10},{3,11},{4,12},{5,13},{6,14},{7,15},{8,0},{9,1},... | collective-permute-start | bytes 196616 | tf_op jit(solution)/shard_map/ppermute | solution.py:461
  73.6 3.4 %collective-permute-start.7 = (f32[128,128]{1,0:T(8,128)S(1)}, f32[128,128]{1,0:T(8,128)S(1)}, u32[]{:S(2)}, u32[]{:S(2)}) collective-permute-start(f32[128,128]{1,0:T(8,128)S(1)} %get-tuple-element.26), channel_id=1, source_target_pairs={{0,12},{1,13},{2,14},{3,15},{4,0},{5,1},{6,2},{7,3},{8,4},{9,5},{1... | collective-permute-start | bytes 196616 | tf_op jit(solution)/shard_map/ppermute | solution.py:461
  75.0 27.4 %copy-start.3 = (f32[2,512,512]{2,1,0:T(8,128)S(1)}, f32[2,512,512]{2,1,0:T(8,128)}, u32[]{:S(2)}) copy-start(f32[2,512,512]{2,1,0:T(8,128)} %copy-done.2) | copy-start | bytes 6291460
  77.0 8.5 %collective-permute-start.10 = (f32[128,128]{1,0:T(8,128)S(1)}, f32[128,128]{1,0:T(8,128)S(1)}, u32[]{:S(2)}, u32[]{:S(2)}) collective-permute-start(f32[128,128]{1,0:T(8,128)S(1)} %y_sum.1.own), channel_id=1, source_target_pairs={{0,3},{1,0},{2,1},{3,2},{4,7},{5,4},{6,5},{7,6},{8,11},{9,8},{10,9... | collective-permute-start | bytes 196616 | tf_op jit(solution)/shard_map/ppermute | solution.py:465
  84.2 6.3 %collective-permute-start.8 = (f32[128,128]{1,0:T(8,128)S(1)}, f32[128,128]{1,0:T(8,128)S(1)}, u32[]{:S(2)}, u32[]{:S(2)}) collective-permute-start(f32[128,128]{1,0:T(8,128)S(1)} %y_sum.1.own), channel_id=1, source_target_pairs={{0,1},{1,2},{2,3},{3,0},{4,5},{5,6},{6,7},{7,4},{8,9},{9,10},{10,1... | collective-permute-start | bytes 196616 | tf_op jit(solution)/shard_map/ppermute | solution.py:465
  84.2 6.3 %collective-permute-start.9 = (f32[128,128]{1,0:T(8,128)S(1)}, f32[128,128]{1,0:T(8,128)S(1)}, u32[]{:S(2)}, u32[]{:S(2)}) collective-permute-start(f32[128,128]{1,0:T(8,128)S(1)} %y_sum.1.own), channel_id=1, source_target_pairs={{0,2},{1,3},{2,0},{3,1},{4,6},{5,7},{6,4},{7,5},{8,10},{9,11},{10,... | collective-permute-start | bytes 196616 | tf_op jit(solution)/shard_map/ppermute | solution.py:465
  90.6 11.7 %collective-permute-start.13 = (f32[2,256,256]{2,1,0:T(8,128)S(1)}, f32[2,256,256]{2,1,0:T(8,128)S(1)}, u32[]{:S(2)}, u32[]{:S(2)}) collective-permute-start(f32[2,256,256]{2,1,0:T(8,128)S(1)} %get-tuple-element.30), channel_id=1, source_target_pairs={{0,1},{1,2},{2,3},{3,4},{4,5},{5,6},{6,7},{7,8},{8,9},{9,10},{10,1... | collective-permute-start | bytes 1572872 | tf_op jit(solution)/shard_map/ppermute | solution.py:449
  92.0 5.1 %collective-permute-start.14 = (f32[128,128]{1,0:T(8,128)S(1)}, f32[128,128]{1,0:T(8,128)S(1)}, u32[]{:S(2)}, u32[]{:S(2)}) collective-permute-start(f32[128,128]{1,0:T(8,128)S(1)} %get-tuple-element.32.own), channel_id=1, source_target_pairs={{0,32},{16,48},{32,64},{48,80},{64,96},{80,112},{96,0},{112,16},{1... | collective-permute-start | bytes 196616 | tf_op jit(solution)/shard_map/ppermute | solution.py:457
  92.0 5.0 %collective-permute-start.15 = (f32[128,128]{1,0:T(8,128)S(1)}, f32[128,128]{1,0:T(8,128)S(1)}, u32[]{:S(2)}, u32[]{:S(2)}) collective-permute-start(f32[128,128]{1,0:T(8,128)S(1)} %get-tuple-element.32.own), channel_id=1, source_target_pairs={{0,64},{16,80},{32,96},{48,112},{64,0},{80,16},{96,32},{112,48},{1... | collective-permute-start | bytes 196616 | tf_op jit(solution)/shard_map/ppermute | solution.py:457
  92.1 5.8 %collective-permute-start.16 = (f32[128,128]{1,0:T(8,128)S(1)}, f32[128,128]{1,0:T(8,128)S(1)}, u32[]{:S(2)}, u32[]{:S(2)}) collective-permute-start(f32[128,128]{1,0:T(8,128)S(1)} %get-tuple-element.32.own), channel_id=1, source_target_pairs={{0,96},{16,112},{32,0},{48,16},{64,32},{80,48},{96,64},{112,80},{1... | collective-permute-start | bytes 196616 | tf_op jit(solution)/shard_map/ppermute | solution.py:457
  98.0 6.0 %collective-permute-start.17 = (f32[128,128]{1,0:T(8,128)S(1)}, f32[128,128]{1,0:T(8,128)S(1)}, u32[]{:S(2)}, u32[]{:S(2)}) collective-permute-start(f32[128,128]{1,0:T(8,128)S(1)} %x_sum.1.own), channel_id=1, source_target_pairs={{0,4},{1,5},{2,6},{3,7},{4,8},{5,9},{6,10},{7,11},{8,12},{9,13},{1... | collective-permute-start | bytes 196616 | tf_op jit(solution)/shard_map/ppermute | solution.py:461
  98.0 5.9 %collective-permute-start.18 = (f32[128,128]{1,0:T(8,128)S(1)}, f32[128,128]{1,0:T(8,128)S(1)}, u32[]{:S(2)}, u32[]{:S(2)}) collective-permute-start(f32[128,128]{1,0:T(8,128)S(1)} %x_sum.1.own), channel_id=1, source_target_pairs={{0,8},{1,9},{2,10},{3,11},{4,12},{5,13},{6,14},{7,15},{8,0},{9,1},... | collective-permute-start | bytes 196616 | tf_op jit(solution)/shard_map/ppermute | solution.py:461
  99.9 4.1 %collective-permute-start.19 = (f32[128,128]{1,0:T(8,128)S(1)}, f32[128,128]{1,0:T(8,128)S(1)}, u32[]{:S(2)}, u32[]{:S(2)}) collective-permute-start(f32[128,128]{1,0:T(8,128)S(1)} %x_sum.1.own), channel_id=1, source_target_pairs={{0,12},{1,13},{2,14},{3,15},{4,0},{5,1},{6,2},{7,3},{8,4},{9,5},{1... | collective-permute-start | bytes 196616 | tf_op jit(solution)/shard_map/ppermute | solution.py:461
  104.5 6.4 %collective-permute-start.20 = (f32[4,128,128]{2,1,0:T(8,128)S(1)}, f32[4,128,128]{2,1,0:T(8,128)S(1)}, u32[]{:S(2)}, u32[]{:S(2)}) collective-permute-start(f32[4,128,128]{2,1,0:T(8,128)S(1)} %half.1), channel_id=1, source_target_pairs={{0,16},{16,0},{32,48},{48,32},{64,80},{80,64},{96,112},{112,96},{1... | collective-permute-start | bytes 786440 | tf_op jit(solution)/shard_map/ppermute | solution.py:453
  (7 other events, 33.5 us)

commit v3 on v2

--- a/solution.py
+++ b/solution.py
@@ -194,29 +194,44 @@
                     pacc_ref[plane, 2 + half, part, :] += jnp.where(lane < HALF - turn, rolled[1], rolled[0])
 
 
-def slot_loop(pairs, local, count_ref, top_ref, left_ref, order, refs):
+EARLY = 4
+
+
+def own_count(counts_ref):
+    return counts_ref[lax.axis_index("row") * lax.axis_size("col") + lax.axis_index("col")]
+
+
+def slot_loop(pairs, stage, counts_ref, positions_ref, order, refs):
     lane = lax.broadcasted_iota(jnp.int32, (ROWS, HALF), 1)
-
-    def enlist(s, n):
-        inside = (top_ref[s] <= PIX) & (left_ref[s] <= PIX)
-        mine = inside if local else jnp.logical_not(inside)
+    above, before = lax.axis_index("row") * 512, lax.axis_index("col") * 512
+
+    def enlist(s, carry):
+        n, early = carry
+        beside = positions_ref[1, s] - before <= PIX
+        first = beside & (positions_ref[0, s] - above <= PIX) & (early < EARLY)
+        if stage == 0:
+            mine = first
+        elif stage == 1:
+            mine = beside & jnp.logical_not(first)
+        else:
+            mine = jnp.logical_not(beside)
 
         @pl.when(mine)
         def _():
             order[n] = s
 
-        return n + mine.astype(jnp.int32)
-
-    total = lax.fori_loop(jnp.int32(0), count_ref[0], enlist, jnp.int32(0))
+        return n + mine.astype(jnp.int32), early + first.astype(jnp.int32)
+
+    total, _ = lax.fori_loop(jnp.int32(0), own_count(counts_ref), enlist, (jnp.int32(0), jnp.int32(0)))
 
     def body(step, carry):
         group = []
         for p in range(pairs):
             place = step * pairs + p
             index = order[jnp.minimum(place, total - 1)]
-            left = left_ref[index]
+            top, left = positions_ref[0, index] - above, positions_ref[1, index] - before
             group.append(dict(
-                p=p, index=index, live=place < total, top=top_ref[index], tile=left // HALF, turn=left % HALF,
+                p=p, index=index, live=place < total, top=top, tile=left // HALF, turn=left % HALF,
             ))
         slot_group(group, lane, *refs)
         return carry
@@ -224,58 +239,89 @@
     lax.fori_loop(jnp.int32(0), (total + pairs - 1) // pairs, body, jnp.int32(0))
 
 
-def order_kernel(count_ref, measured_ref, ordered_out, raw, sems):
-    copies = [
-        pltpu.make_async_copy(measured_ref.at[:, :, pl.ds(t * HALF, HALF)], raw.at[t], sems.at[t])
-        for t in range(2)
+def early_kernel(
+    pairs,
+    counts_ref, positions_ref, measured_ref, object_ref, probe_ref, table_ref,
+    ordered_out, acc_out, pacc_out,
+    raw, ext, order, sems, tile_sems, *work,
+):
+    tiles = [
+        pltpu.make_async_copy(object_ref.at[:, :, pl.ds(t * HALF, HALF)], ext.at[:, t], tile_sems.at[t])
+        for t in range(TILES)
     ]
-    for copy in copies:
+
+    def coming(s, t):
+        return pltpu.make_async_copy(measured_ref.at[s, :, pl.ds(t * HALF, HALF)], raw.at[s, t], sems.at[s, t])
+
+    for s in range(16):
+        for t in range(2):
+            coming(s, t).start()
+    for copy in tiles:
         copy.start()
+    acc_out[...] = jnp.zeros_like(acc_out)
+    pacc_out[...] = jnp.zeros_like(pacc_out)
     lane = lax.broadcasted_iota(jnp.int32, (HALF, HALF), 1)
     first = lane < 64
     even_first = jnp.where(first, 2 * lane, 2 * lane - 127)
     odd_first = jnp.where(first, 2 * lane + 1, 2 * lane - 128)
-    for copy in copies:
-        copy.wait()
 
     def reorder(s, carry):
+        for t in range(2):
+            coming(s, t).wait()
         for parity in range(2):
             rows = pl.ds(parity, HALF, stride=2)
-            left = jnp.take_along_axis(raw[0, s, rows, :], even_first, axis=1)
-            right = jnp.take_along_axis(raw[1, s, rows, :], odd_first, axis=1)
+            left = jnp.take_along_axis(raw[s, 0, rows, :], even_first, axis=1)
+            right = jnp.take_along_axis(raw[s, 1, rows, :], odd_first, axis=1)
             out = slice(parity * HALF, (parity + 1) * HALF)
             ordered_out[s, out, :HALF] = jnp.where(first, left, right)
             ordered_out[s, out, HALF:] = pltpu.roll(jnp.where(first, right, left), 64, 1)
         return carry
 
-    lax.fori_loop(jnp.int32(0), count_ref[0], reorder, jnp.int32(0))
+    def skip(s, carry):
+        for t in range(2):
+            coming(s, t).wait()
+        return carry
+
+    count = own_count(counts_ref)
+    lax.fori_loop(jnp.int32(0), count, reorder, jnp.int32(0))
+    lax.fori_loop(count, jnp.int32(16), skip, jnp.int32(0))
+    for copy in tiles:
+        copy.wait()
+    slot_loop(
+        pairs, 0, counts_ref, positions_ref, order,
+        (ext, acc_out, pacc_out, probe_ref, ordered_out, table_ref, work),
+    )
 
 
 def local_kernel(
     pairs,
-    count_ref, top_ref, left_ref, object_ref, ordered_ref, probe_ref, table_ref,
+    counts_ref, positions_ref, object_ref, lower_rim, held_ref, pacc_ref, ordered_ref, probe_ref, table_ref,
     acc_out, pacc_out,
     ext, order, sems, *work,
 ):
-    copies = [
-        pltpu.make_async_copy(object_ref.at[:, :, pl.ds(t * HALF, HALF)], ext.at[:, t], sems.at[t])
-        for t in range(TILES)
-    ]
+    copies = []
+    for t in range(TILES):
+        cols = pl.ds(t * HALF, HALF)
+        copies.append(pltpu.make_async_copy(object_ref.at[:, :, cols], ext.at[:, t, pl.ds(0, 512)], sems.at[2 * t]))
+        copies.append(
+            pltpu.make_async_copy(lower_rim.at[:, :, cols], ext.at[:, t, pl.ds(512, PIX)], sems.at[2 * t + 1])
+        )
     for copy in copies:
         copy.start()
-    acc_out[...] = jnp.zeros_like(acc_out)
-    pacc_out[...] = jnp.zeros_like(pacc_out)
+    acc_out[:, :, 0:512, :] = held_ref[...]
+    acc_out[:, :, 512:768, :] = jnp.zeros((2, TILES + 1, PIX, HALF), F32)
+    pacc_out[...] = pacc_ref[...]
     for copy in copies:
         copy.wait()
     slot_loop(
-        pairs, True, count_ref, top_ref, left_ref, order,
+        pairs, 1, counts_ref, positions_ref, order,
         (ext, acc_out, pacc_out, probe_ref, ordered_ref, table_ref, work),
     )
 
 
 def rest_kernel(
     pairs,
-    count_ref, top_ref, left_ref, place_ref, object_ref, top_rim, bottom_rim, lower_rim, corner_rim, held_ref,
+    counts_ref, positions_ref, object_ref, top_rim, bottom_rim, lower_rim, corner_rim, held_ref,
     pacc_ref, ordered_ref, probe_ref, table_ref,
     tile_out, top_out, bottom_out, lower_out, mine_out, other_out,
     ext, acc, pacc, order, sems, *work,
@@ -290,39 +336,45 @@
         cols = pl.ds(t * HALF, HALF)
         bring(object_ref.at[:, :, cols], ext.at[:, t, pl.ds(0, 512)])
         bring(lower_rim.at[:, :, cols], ext.at[:, t, pl.ds(512, PIX)])
-        bring(held_ref.at[:, t], acc.at[:, t, pl.ds(0, 512)])
+        bring(held_ref.at[:, t], acc.at[:, t])
     for t in range(2):
         cols = pl.ds(t * HALF, HALF)
         bring(top_rim.at[:, :, cols], ext.at[:, TILES + t, pl.ds(0, PIX)])
         bring(bottom_rim.at[:, :, cols], ext.at[:, TILES + t, pl.ds(PIX, PIX)])
         bring(corner_rim.at[:, :, cols], ext.at[:, TILES + t, pl.ds(512, PIX)])
-    acc[:, 0:TILES, 512:768, :] = jnp.zeros((2, TILES, PIX, HALF), F32)
     acc[:, TILES:, :, :] = jnp.zeros((2, 2, 768, HALF), F32)
     pacc[...] = pacc_ref[...]
     for copy in copies:
         copy.wait()
     slot_loop(
-        pairs, False, count_ref, top_ref, left_ref, order,
+        pairs, 2, counts_ref, positions_ref, order,
         (ext, acc, pacc, probe_ref, ordered_ref, table_ref, work),
     )
-    y_pos, core = place_ref[0], place_ref[1]
+    y_pos, core = lax.axis_index("col") // 4, lax.axis_index("row") % 2
     for k in range(4):
         mine_out[k] = pacc[core, (y_pos + k) % 4]
         other_out[k] = pacc[1 - core, (y_pos + k) % 4]
+    leaving = []
     for t in range(TILES):
-        cols = slice(t * HALF, (t + 1) * HALF)
-        tile_out[:, :, cols] = ext[:, t, 0:512, :] + OBJECT_RATE * acc[:, t, 0:512, :]
+        ext[:, t, 0:512, :] = ext[:, t, 0:512, :] + OBJECT_RATE * acc[:, t, 0:512, :]
+        leaving.append(
+            pltpu.make_async_copy(ext.at[:, t, pl.ds(0, 512)], tile_out.at[:, :, pl.ds(t * HALF, HALF)], sems.at[t])
+        )
+        leaving[-1].start()
     for t in range(TILES + 2):
         lower_out[:, :, t * HALF : (t + 1) * HALF] = OBJECT_RATE * acc[:, t, 512:768, :]
     for t in range(2):
         cols = slice(t * HALF, (t + 1) * HALF)
         top_out[:, :, cols] = OBJECT_RATE * acc[:, TILES + t, 0:PIX, :]
         bottom_out[:, :, cols] = OBJECT_RATE * acc[:, TILES + t, PIX:512, :]
+    for copy in leaving:
+        copy.wait()
 
 
 VMEM = pl.BlockSpec(memory_space=pltpu.VMEM)
 SMEM = pl.BlockSpec(memory_space=pltpu.SMEM)
 ANYWHERE = pl.BlockSpec(memory_space=pl.ANY)
+HBM = pl.BlockSpec(memory_space=pltpu.HBM)
 
 
 def work_shapes(pairs):
@@ -344,43 +396,54 @@
 BLOCK = jax.ShapeDtypeStruct((2, PIX, PIX), F32)
 
 
-def in_order(count, measured):
+def process_early(counts, positions, measured, tile, probe, tables):
+    pairs = 2
     return pl.pallas_call(
-        order_kernel,
-        in_specs=[SMEM, ANYWHERE],
-        out_specs=VMEM,
-        out_shape=jax.ShapeDtypeStruct((16, PIX, PIX), F32),
-        scratch_shapes=[pltpu.VMEM((2, 16, PIX, HALF), F32), pltpu.SemaphoreType.DMA((2,))],
-        compiler_params=pltpu.CompilerParams(vmem_limit_bytes=10 * 1024 * 1024),
-        cost_estimate=pl.CostEstimate(flops=0, bytes_accessed=16 * 2**20, transcendentals=0),
-        name="order_measured",
-    )(count, measured)
-
-
-def process_local(count, tops, lefts, tile, ordered, probe, tables):
+        functools.partial(early_kernel, pairs),
+        in_specs=[SMEM] * 2 + [HBM] * 2 + [VMEM] * 2,
+        out_specs=[VMEM] * 3,
+        out_shape=[
+            jax.ShapeDtypeStruct((16, PIX, PIX), F32),
+            jax.ShapeDtypeStruct((2, TILES + 1, 512, HALF), F32),
+            jax.ShapeDtypeStruct((2, 4, HALF, HALF), F32),
+        ],
+        scratch_shapes=[
+            pltpu.VMEM((16, 2, PIX, HALF), F32),
+            pltpu.VMEM((2, TILES + 1, 512, HALF), F32),
+            pltpu.SMEM((16,), jnp.int32),
+            pltpu.SemaphoreType.DMA((16, 2)),
+            pltpu.SemaphoreType.DMA((TILES,)),
+        ] + work_shapes(pairs),
+        compiler_params=pltpu.CompilerParams(vmem_limit_bytes=26 * 1024 * 1024),
+        cost_estimate=pl.CostEstimate(flops=0, bytes_accessed=2**20, transcendentals=0),
+        name="early_slots",
+    )(counts, positions, measured, tile, probe, tables)
+
+
+def process_local(counts, positions, tile, lower, held, pacc, ordered, probe, tables):
     pairs = 2
     return pl.pallas_call(
         functools.partial(local_kernel, pairs),
-        in_specs=[SMEM] * 3 + [ANYWHERE] + [VMEM] * 3,
+        in_specs=[SMEM] * 2 + [HBM] * 2 + [VMEM] * 5,
         out_specs=[VMEM] * 2,
-        out_shape=[jax.ShapeDtypeStruct((2, TILES + 1, 512, HALF), F32), jax.ShapeDtypeStruct((2, 4, HALF, HALF), F32)],
+        out_shape=[jax.ShapeDtypeStruct((2, TILES + 1, 768, HALF), F32), jax.ShapeDtypeStruct((2, 4, HALF, HALF), F32)],
         scratch_shapes=[
-            pltpu.VMEM((2, TILES + 1, 512, HALF), F32),
+            pltpu.VMEM((2, TILES + 1, 768, HALF), F32),
             pltpu.SMEM((16,), jnp.int32),
-            pltpu.SemaphoreType.DMA((TILES,)),
+            pltpu.SemaphoreType.DMA((2 * TILES,)),
         ] + work_shapes(pairs),
-        compiler_params=pltpu.CompilerParams(vmem_limit_bytes=22 * 1024 * 1024),
+        compiler_params=pltpu.CompilerParams(vmem_limit_bytes=26 * 1024 * 1024),
         cost_estimate=pl.CostEstimate(flops=6 * 10**9, bytes_accessed=20 * 2**20, transcendentals=2**20),
         name="local_slots",
-    )(count, tops, lefts, tile, ordered, probe, tables)
-
-
-def process_rest(count, tops, lefts, place, tile, top, bottom, lower, corner, held, pacc, ordered, probe, tables):
+    )(counts, positions, tile, lower, held, pacc, ordered, probe, tables)
+
+
+def process_rest(counts, positions, tile, top, bottom, lower, corner, held, pacc, ordered, probe, tables):
     pairs = 2
     return pl.pallas_call(
         functools.partial(rest_kernel, pairs),
-        in_specs=[SMEM] * 4 + [ANYWHERE] * 6 + [VMEM] * 4,
-        out_specs=[VMEM] * 6,
+        in_specs=[SMEM] * 2 + [HBM] * 5 + [ANYWHERE] + [VMEM] * 4,
+        out_specs=[HBM] + [VMEM] * 5,
         out_shape=[WHOLE_TILE] + [BLOCK] * 2 + [LOWER] + [QUARTERS] * 2,
         scratch_shapes=[
             pltpu.VMEM((2, TILES + 2, 768, HALF), F32),
@@ -392,7 +455,7 @@
         compiler_params=pltpu.CompilerParams(vmem_limit_bytes=30 * 1024 * 1024),
         cost_estimate=pl.CostEstimate(flops=13 * 10**9, bytes_accessed=20 * 2**20, transcendentals=2**20),
         name="other_slots",
-    )(count, tops, lefts, place, tile, top, bottom, lower, corner, held, pacc, ordered, probe, tables)
+    )(counts, positions, tile, top, bottom, lower, corner, held, pacc, ordered, probe, tables)
 
 
 def joined(kernel, name, operands, outs, smem=0, beside=()):
@@ -429,13 +492,14 @@
     token[...] = jnp.zeros_like(token)
 
 
-def half_kernel(place_ref, own, one, two, three, token, half):
+def half_kernel(own, one, two, three, token, half):
     for k, part in enumerate((own, one, two, three)):
-        half[(place_ref[0] + 4 - k) % 4] = part[...]
-
-
-def probe_kernel(place_ref, root_ref, probe, half, other, out):
-    core, root = place_ref[1], root_ref[0]
+        half[(lax.axis_index("col") // 4 + 4 - k) % 4] = part[...]
+
+
+def probe_kernel(counts, probe, half, other, out):
+    core = lax.axis_index("row") % 2
+    root = jnp.sqrt(jnp.sum(counts[...].astype(F32), axis=1, keepdims=True))
     for q in range(4):
         at = (slice(q % 2 * HALF, (q % 2 + 1) * HALF), slice(q // 2 * HALF, (q // 2 + 1) * HALF))
         mine, theirs = half[q], other[q]
@@ -466,28 +530,22 @@
 
 
 def per_device(object_field, probe_field, measured, positions, counts):
-    row_pos = lax.axis_index("row")
-    col_pos = lax.axis_index("col")
-    own_device = row_pos * lax.axis_size("col") + col_pos
-    place = jnp.stack([col_pos // 4, row_pos % 2])
-    root = jnp.sqrt(jnp.sum(counts).astype(F32))[None]
     tables = jnp.asarray(dft_tables())
     top = passed_along(object_field[:, :PIX, :PIX], "col", -1)
     bottom = passed_along(object_field[:, PIX:, :PIX], "col", -1)
     lower = passed_along(object_field[:, :PIX, :], "row", -1)
     corner = passed_along(top, "row", -1)
-    count = counts[own_device][None]
-    where = (count, positions[:, 0] - row_pos * 512, positions[:, 1] - col_pos * 512)
-    ordered = in_order(count, measured)
-    held, pacc = process_local(*where, object_field, ordered, probe_field, tables)
+    where = (counts, positions.T)
+    ordered, held, pacc = process_early(*where, measured, object_field, probe_field, tables)
+    held, pacc = process_local(*where, object_field, lower, held, pacc, ordered, probe_field, tables)
     tile, top_sum, bottom_sum, lower_sum, mine, other = process_rest(
-        *where, place, object_field, top, bottom, lower, corner, held, pacc, ordered, probe_field, tables
+        *where, object_field, top, bottom, lower, corner, held, pacc, ordered, probe_field, tables
     )
     lower_back = passed_along(lower_sum, "row", 1)
     bottom_back = passed_along(bottom_sum, "col", 1)
     quarters = joined(pair_kernel, "pair_sum", (mine, over_core(other)), [QUARTER] * 4)
     (part,) = joined(
-        ring_kernel, "y_sum", [quarters[0]] + [over_y(quarters[k], k) for k in (1, 2, 3)], [QUARTER], beside=[root]
+        ring_kernel, "y_sum", [quarters[0]] + [over_y(quarters[k], k) for k in (1, 2, 3)], [QUARTER]
     )
     part, rim = joined(
         corner_kernel, "z_sum", [part] + [over_z(part, k) for k in (1, 2, 3)] + [top_sum, lower_back],
@@ -499,11 +557,11 @@
         tile_kernel, "new_tile", (tile, top_back, bottom_back, lower_back), [WHOLE_TILE, TOKEN]
     )
     (half,) = joined(
-        half_kernel, "half", [place, part] + [over_y(part, k) for k in (1, 2, 3)], [QUARTERS], smem=1,
+        half_kernel, "half", [part] + [over_y(part, k) for k in (1, 2, 3)], [QUARTERS],
         beside=[token],
     )
     (new_probe,) = joined(
-        probe_kernel, "new_probe", (place, root, probe_field, half, over_core(half)), [BLOCK], smem=2,
+        probe_kernel, "new_probe", (counts[None], probe_field, half, over_core(half)), [BLOCK],
     )
     return (new_object, new_probe)
 

time: 114 us -> 108 us (0.947); the launches traced: 112 us -> 108 us
  local copies, waits for them, and re-layouts: 8.67 us -> 3.76 us
  starting transfers between devices: 47.1 us -> 48.8 us
    ppermute x3, starting transfers between devices: 8.46 us -> 11.3 us  [over_z(): lax.ppermute(v, 'col', [(i, i // 4 * 4 + (i % 4 + k) % 4) for i in range(...]
    pallas_call x1, Pallas kernels: 7.7 us -> 10.4 us  [process_local(): pl.pallas_call(functools.partial(local_kernel, pairs), in_specs=[SMEM] *...]
    unnamed x20 -> x12, local copies, waits for them, and re-layouts: 4.57 us -> 2.21 us
    slice x1, local copies, waits for them, and re-layouts: 2.41 us -> 0.1 us  [per_device(): bottom = passed_along(object_field[:, PIX:, :PIX], 'col', -1)]
    ppermute x6, starting transfers between devices: 15.6 us -> 13.5 us  [over_y(): return lax.ppermute(v, 'col', [(i, (i + 4 * k) % 16) for i in range(16)])]
    ppermute x3, starting transfers between devices: 2.73 us -> 4.81 us  [over_x(): return lax.ppermute(v, 'row', [(i, (i + 2 * k) % 8) for i in range(8)])]
    ppermute x7, waiting for transfers between devices: 1.83 us -> 0.02 us  [passed_along(): return lax.ppermute(shard, axis, pairs)]
    pallas_call x7, Pallas kernels: 4.33 us -> 2.73 us  [joined(): pl.pallas_call(kernel, in_specs=[SMEM] * smem + [VMEM] * (len(operands) -...]
  transfers between devices with their start and end apart: 21 -> 21, of which waited for: 11 -> 9; matrix products, arithmetic and copies ran while one was open for 2% -> 0% of each run, Pallas kernels for 14% -> 22%
where the time goes in v3:
time: 108 us
  starting transfers between devices  48.8 us (45%)
  Pallas kernels  39.6 us (37%)
  waiting for transfers between devices  14.6 us (14%)
  local copies, waits for them, and re-layouts  3.76 us (3%)
    pallas_call x1, Pallas kernels, process_rest(): pl.pallas_call(functools.partial(rest_kernel, pairs), in_specs=[SMEM] * 2...  14.4 us
    ppermute x7, starting transfers between devices, passed_along(): return lax.ppermute(shard, axis, pairs)  14.3 us
    ppermute x6, starting transfers between devices, over_y(): return lax.ppermute(v, 'col', [(i, (i + 4 * k) % 16) for i in range(16)])  13.5 us
    pallas_call x1, Pallas kernels, process_early(): pl.pallas_call(functools.partial(early_kernel, pairs), in_specs=[SMEM] *...  12.1 us
    ppermute x3, starting transfers between devices, over_z(): lax.ppermute(v, 'col', [(i, i // 4 * 4 + (i % 4 + k) % 4) for i in range(...  11.3 us
    pallas_call x1, Pallas kernels, process_local(): pl.pallas_call(functools.partial(local_kernel, pairs), in_specs=[SMEM] *...  10.4 us
    ppermute x2, starting transfers between devices, over_core(): return lax.ppermute(v, 'row', [(i, i ^ 1) for i in range(8)])  4.93 us
    ppermute x3, starting transfers between devices, over_x(): return lax.ppermute(v, 'row', [(i, (i + 2 * k) % 8) for i in range(8)])  4.81 us
  transfers between devices with their start and end apart: 21, of which 9 were waited for; matrix products, arithmetic and copies ran while one was open for 0% of the time, Pallas kernels for 22%

profile of v3, /device:TPU:1, one launch (start us, length us, event | category | flops | bytes accessed | tf_op | source)
XLA Modules:
  0.0 107.7 jit_solution(11120125725243117203)
XLA Ops:
  0.7 1.4 %slice.11 = f32[2,256,512]{2,1,0:T(8,128)S(1)} slice(f32[2,512,512]{2,1,0:T(8,128)} %object_ref.5), slice={[0:2], [0:256], [0:512]} | slice | bytes 2097152 | tf_op jit(solution)/shard_map/slice | solution.py:536
  2.1 3.3 %collective-permute-start.2 = (f32[2,256,512]{2,1,0:T(8,128)S(1)}, f32[2,256,512]{2,1,0:T(8,128)S(1)}, u32[]{:S(2)}, u32[]{:S(2)}) collective-permute-start(f32[2,256,512]{2,1,0:T(8,128)S(1)} %slice.11), channel_id=1, source_target_pairs={{16,0},{32,16},{48,32},{64,48},{80,64},{96,80},{112,96},{17,1},{33... | collective-permute-start | bytes 3145736 | tf_op jit(solution)/shard_map/ppermute | solution.py:513
  5.6 1.3 %collective-permute-start = (f32[2,256,256]{2,1,0:T(8,128)S(1)}, f32[2,256,256]{2,1,0:T(8,128)S(1)}, u32[]{:S(2)}, u32[]{:S(2)}) collective-permute-start(f32[2,256,256]{2,1,0:T(8,128)S(1)} %get-tuple-element.41), channel_id=1, source_target_pairs={{1,0},{2,1},{3,2},{4,3},{5,4},{6,5},{7,6},{8,7},{9,8},{10,9},{11,1... | collective-permute-start | bytes 1572872 | tf_op jit(solution)/shard_map/ppermute | solution.py:513
  6.9 1.3 %collective-permute-start.1 = (f32[2,256,256]{2,1,0:T(8,128)S(1)}, f32[2,256,256]{2,1,0:T(8,128)S(1)}, u32[]{:S(2)}, u32[]{:S(2)}) collective-permute-start(f32[2,256,256]{2,1,0:T(8,128)S(1)} %get-tuple-element.40), channel_id=1, source_target_pairs={{1,0},{2,1},{3,2},{4,3},{5,4},{6,5},{7,6},{8,7},{9,8},{10,9},{11,1... | collective-permute-start | bytes 1572872 | tf_op jit(solution)/shard_map/ppermute | solution.py:513
  8.2 2.2 %copy-done.1 = f32[16,256,256]{2,1,0:T(8,128)S(1)} copy-done((f32[16,256,256]{2,1,0:T(8,128)S(1)}, f32[16,256,256]{2,1,0:T(8,128)}, u32[]{:S(2)}) %copy-start.1) | copy-done | bytes 4194328
  10.4 12.1 %early_slots.1 = (f32[16,256,256]{2,1,0:T(8,128)S(1)}, f32[2,5,512,128]{3,2,1,0:T(8,128)S(1)}, f32[2,4,128,128]{3,2,1,0:T(8,128)S(1)}) custom-call(s32[128]{0:T(128)S(1)} %copy-done.4, s32[2,16]{1,0:T(2,128)S(1)} %bitcast.3, f32[16,256,256]{2,1,0:T(8,128)S(1)} %copy-done.1, f32[2,512,512]{2,1,0:T(8,128)S(1)} %copy-done, f32[2,256,256]{2,1,0:T(8,128)S(1)} %copy-done.2, ...), custom_call_target="tpu_custom_call" | custom-call | bytes 1048576 | tf_op jit(solution)/shard_map/early_slots/pallas_call | solution.py:401
  22.6 1.9 %collective-permute-start.3 = (f32[2,256,256]{2,1,0:T(8,128)S(1)}, f32[2,256,256]{2,1,0:T(8,128)S(1)}, u32[]{:S(2)}, u32[]{:S(2)}) collective-permute-start(f32[2,256,256]{2,1,0:T(8,128)S(1)} %collective-permute-done.top_rim), channel_id=1, source_target_pairs={{16,0},{32,16},{48,32},{64,48},{80,64},{96,80},{112,96},{17,1},{33... | collective-permute-start | bytes 1572872 | tf_op jit(solution)/shard_map/ppermute | solution.py:513
  24.5 10.4 %local_slots.1 = (f32[2,5,768,128]{3,2,1,0:T(8,128)S(1)}, f32[2,4,128,128]{3,2,1,0:T(8,128)S(1)}) custom-call(s32[128]{0:T(128)S(1)} %copy-done.4, s32[2,16]{1,0:T(2,128)S(1)} %bitcast.4, f32[2,512,512]{2,1,0:T(8,128)S(1)} %copy-done, f32[2,256,512]{2,1,0:T(8,128)S(1)} %collective-permute-done.2.lower_rim, ...), custom_call_target="tpu_custom_call" | custom-call | flops 6000000000 | bytes 20971520 | tf_op jit(solution)/shard_map/local_slots/pallas_call | solution.py:425
  34.9 14.4 %other_slots.1 = (f32[2,512,512]{2,1,0:T(8,128)S(1)}, f32[2,256,256]{2,1,0:T(8,128)S(1)}, f32[2,256,256]{2,1,0:T(8,128)S(1)}, f32[2,256,768]{2,1,0:T(8,128)S(1)}...) custom-call(s32[128]{0:T(128)S(1)} %copy-done.4, s32[2,16]{1,0:T(2,128)S(1)} %bitcast.5, ...), custom_call_target="tpu_custom_call" | custom-call | flops 12999999488 | bytes 20971520 | tf_op jit(solution)/shard_map/other_slots/pallas_call | solution.py:443
  49.3 2.1 %collective-permute-start.11 = (f32[2,256,768]{2,1,0:T(8,128)S(1)}, f32[2,256,768]{2,1,0:T(8,128)S(1)}, u32[]{:S(2)}, u32[]{:S(2)}) collective-permute-start(f32[2,256,768]{2,1,0:T(8,128)S(1)} %get-tuple-element.34), channel_id=1, source_target_pairs={{0,16},{16,32},{32,48},{48,64},{64,80},{80,96},{96,112},{1,17},{17... | collective-permute-start | bytes 4718600 | tf_op jit(solution)/shard_map/ppermute | solution.py:513
  51.4 3.1 %collective-permute-start.12 = (f32[2,256,256]{2,1,0:T(8,128)S(1)}, f32[2,256,256]{2,1,0:T(8,128)S(1)}, u32[]{:S(2)}, u32[]{:S(2)}) collective-permute-start(f32[2,256,256]{2,1,0:T(8,128)S(1)} %get-tuple-element.35), channel_id=1, source_target_pairs={{0,1},{1,2},{2,3},{3,4},{4,5},{5,6},{6,7},{7,8},{8,9},{9,10},{10,1... | collective-permute-start | bytes 1572872 | tf_op jit(solution)/shard_map/ppermute | solution.py:513
  56.6 3.2 %collective-permute-start.5 = (f32[128,128]{1,0:T(8,128)S(1)}, f32[128,128]{1,0:T(8,128)S(1)}, u32[]{:S(2)}, u32[]{:S(2)}) collective-permute-start(f32[128,128]{1,0:T(8,128)S(1)} %get-tuple-element.30), channel_id=1, source_target_pairs={{0,4},{1,5},{2,6},{3,7},{4,8},{5,9},{6,10},{7,11},{8,12},{9,13},{1... | collective-permute-start | bytes 196616 | tf_op jit(solution)/shard_map/ppermute | solution.py:525
  59.8 5.1 %collective-permute-start.6 = (f32[128,128]{1,0:T(8,128)S(1)}, f32[128,128]{1,0:T(8,128)S(1)}, u32[]{:S(2)}, u32[]{:S(2)}) collective-permute-start(f32[128,128]{1,0:T(8,128)S(1)} %get-tuple-element.31), channel_id=1, source_target_pairs={{0,8},{1,9},{2,10},{3,11},{4,12},{5,13},{6,14},{7,15},{8,0},{9,1},... | collective-permute-start | bytes 196616 | tf_op jit(solution)/shard_map/ppermute | solution.py:525
  65.0 2.0 %collective-permute-start.7 = (f32[128,128]{1,0:T(8,128)S(1)}, f32[128,128]{1,0:T(8,128)S(1)}, u32[]{:S(2)}, u32[]{:S(2)}) collective-permute-start(f32[128,128]{1,0:T(8,128)S(1)} %get-tuple-element.32), channel_id=1, source_target_pairs={{0,12},{1,13},{2,14},{3,15},{4,0},{5,1},{6,2},{7,3},{8,4},{9,5},{1... | collective-permute-start | bytes 196616 | tf_op jit(solution)/shard_map/ppermute | solution.py:525
  66.9 1.5 %collective-permute-done.6.two = f32[128,128]{1,0:T(8,128)S(1)} collective-permute-done((f32[128,128]{1,0:T(8,128)S(1)}, f32[128,128]{1,0:T(8,128)S(1)}, u32[]{:S(2)}, u32[]{:S(2)}) %collective-permute-start.6) | collective-permute-done | bytes 65568 | tf_op jit(solution)/shard_map/ppermute | solution.py:525
  68.4 10.6 %collective-permute-start.10 = (f32[128,128]{1,0:T(8,128)S(1)}, f32[128,128]{1,0:T(8,128)S(1)}, u32[]{:S(2)}, u32[]{:S(2)}) collective-permute-start(f32[128,128]{1,0:T(8,128)S(1)} %y_sum.1.own), channel_id=1, source_target_pairs={{0,3},{1,0},{2,1},{3,2},{4,7},{5,4},{6,5},{7,6},{8,11},{9,8},{10,9... | collective-permute-start | bytes 196616 | tf_op jit(solution)/shard_map/ppermute | solution.py:529
  81.0 2.8 %collective-permute-done.9.two = f32[128,128]{1,0:T(8,128)S(1)} collective-permute-done((f32[128,128]{1,0:T(8,128)S(1)}, f32[128,128]{1,0:T(8,128)S(1)}, u32[]{:S(2)}, u32[]{:S(2)}) %collective-permute-start.9) | collective-permute-done | bytes 65568 | tf_op jit(solution)/shard_map/ppermute | solution.py:529
  84.2 1.3 %collective-permute-start.13 = (f32[2,256,256]{2,1,0:T(8,128)S(1)}, f32[2,256,256]{2,1,0:T(8,128)S(1)}, u32[]{:S(2)}, u32[]{:S(2)}) collective-permute-start(f32[2,256,256]{2,1,0:T(8,128)S(1)} %get-tuple-element.36), channel_id=1, source_target_pairs={{0,1},{1,2},{2,3},{3,4},{4,5},{5,6},{6,7},{7,8},{8,9},{9,10},{10,1... | collective-permute-start | bytes 1572872 | tf_op jit(solution)/shard_map/ppermute | solution.py:513
  85.6 4.0 %collective-permute-start.15 = (f32[128,128]{1,0:T(8,128)S(1)}, f32[128,128]{1,0:T(8,128)S(1)}, u32[]{:S(2)}, u32[]{:S(2)}) collective-permute-start(f32[128,128]{1,0:T(8,128)S(1)} %get-tuple-element.38.own), channel_id=1, source_target_pairs={{0,64},{16,80},{32,96},{48,112},{64,0},{80,16},{96,32},{112,48},{1... | collective-permute-start | bytes 196616 | tf_op jit(solution)/shard_map/ppermute | solution.py:521
  91.2 3.5 %collective-permute-done.14.one = f32[128,128]{1,0:T(8,128)S(1)} collective-permute-done((f32[128,128]{1,0:T(8,128)S(1)}, f32[128,128]{1,0:T(8,128)S(1)}, u32[]{:S(2)}, u32[]{:S(2)}) %collective-permute-start.14) | collective-permute-done | bytes 65568 | tf_op jit(solution)/shard_map/ppermute | solution.py:521
  94.8 2.3 %collective-permute-start.18 = (f32[128,128]{1,0:T(8,128)S(1)}, f32[128,128]{1,0:T(8,128)S(1)}, u32[]{:S(2)}, u32[]{:S(2)}) collective-permute-start(f32[128,128]{1,0:T(8,128)S(1)} %x_sum.1.own), channel_id=1, source_target_pairs={{0,8},{1,9},{2,10},{3,11},{4,12},{5,13},{6,14},{7,15},{8,0},{9,1},... | collective-permute-start | bytes 196616 | tf_op jit(solution)/shard_map/ppermute | solution.py:525
  98.0 1.6 %new_tile.1 = (f32[2,512,512]{2,1,0:T(8,128)}, f32[8,128]{1,0:T(8,128)S(1)}) custom-call(f32[2,512,512]{2,1,0:T(8,128)S(1)} %get-tuple-element.26.tile, f32[2,256,256]{2,1,0:T(8,128)S(1)} %collective-permute-done.13.top, f32[2,256,256]{2,1,0:T(8,128)S(1)} %collective-permute-done.12.bottom, f32[2,256,768]{2,1,0:T(8,128)S(1)} %collective-permute-done.11.lower), custom_call_target="tpu_custom_call" | custom-call | flops 262144 | bytes 1048576 | tf_op jit(solution)/shard_map/new_tile/pallas_call | solution.py:462
  99.6 2.0 %collective-permute-done.17.one = f32[128,128]{1,0:T(8,128)S(1)} collective-permute-done((f32[128,128]{1,0:T(8,128)S(1)}, f32[128,128]{1,0:T(8,128)S(1)}, u32[]{:S(2)}, u32[]{:S(2)}) %collective-permute-start.17) | collective-permute-done | bytes 65568 | tf_op jit(solution)/shard_map/ppermute | solution.py:525
  101.5 4.0 %collective-permute-start.20 = (f32[4,128,128]{2,1,0:T(8,128)S(1)}, f32[4,128,128]{2,1,0:T(8,128)S(1)}, u32[]{:S(2)}, u32[]{:S(2)}) collective-permute-start(f32[4,128,128]{2,1,0:T(8,128)S(1)} %half.1), channel_id=1, source_target_pairs={{0,16},{16,0},{32,48},{48,32},{64,80},{80,64},{96,112},{112,96},{1... | collective-permute-start | bytes 786440 | tf_op jit(solution)/shard_map/ppermute | solution.py:517
  (42 shorter events, 9.4 us)
Async XLA Ops:
  0.6 7.6 %copy-start.3 = (bf16[8,256,256]{2,1,0:T(8,128)(2,1)S(1)}, bf16[8,256,256]{2,1,0:T(8,128)(2,1)}, u32[]{:S(2)}) copy-start(bf16[8,256,256]{2,1,0:T(8,128)(2,1)} %constant.2.clone.table_ref) | copy-start | bytes 3145732
  0.7 7.6 %copy-start.4 = (s32[128]{0:T(128)S(1)}, s32[128]{0:T(128)}, u32[]{:S(2)}) copy-start(s32[128]{0:T(128)} %counts_ref.5) | copy-start | bytes 1540
  0.7 7.6 %copy-start.2 = (f32[2,256,256]{2,1,0:T(8,128)S(1)}, f32[2,256,256]{2,1,0:T(8,128)}, u32[]{:S(2)}) copy-start(f32[2,256,256]{2,1,0:T(8,128)} %probe.1) | copy-start | bytes 1572868
  2.1 22.4 %collective-permute-start.2 = (f32[2,256,512]{2,1,0:T(8,128)S(1)}, f32[2,256,512]{2,1,0:T(8,128)S(1)}, u32[]{:S(2)}, u32[]{:S(2)}) collective-permute-start(f32[2,256,512]{2,1,0:T(8,128)S(1)} %slice.11), channel_id=1, source_target_pairs={{16,0},{32,16},{48,32},{64,48},{80,64},{96,80},{112,96},{17,1},{33... | collective-permute-start | bytes 3145736 | tf_op jit(solution)/shard_map/ppermute | solution.py:513
  5.6 17.0 %collective-permute-start = (f32[2,256,256]{2,1,0:T(8,128)S(1)}, f32[2,256,256]{2,1,0:T(8,128)S(1)}, u32[]{:S(2)}, u32[]{:S(2)}) collective-permute-start(f32[2,256,256]{2,1,0:T(8,128)S(1)} %get-tuple-element.41), channel_id=1, source_target_pairs={{1,0},{2,1},{3,2},{4,3},{5,4},{6,5},{7,6},{8,7},{9,8},{10,9},{11,1... | collective-permute-start | bytes 1572872 | tf_op jit(solution)/shard_map/ppermute | solution.py:513
  6.9 28.0 %collective-permute-start.1 = (f32[2,256,256]{2,1,0:T(8,128)S(1)}, f32[2,256,256]{2,1,0:T(8,128)S(1)}, u32[]{:S(2)}, u32[]{:S(2)}) collective-permute-start(f32[2,256,256]{2,1,0:T(8,128)S(1)} %get-tuple-element.40), channel_id=1, source_target_pairs={{1,0},{2,1},{3,2},{4,3},{5,4},{6,5},{7,6},{8,7},{9,8},{10,9},{11,1... | collective-permute-start | bytes 1572872 | tf_op jit(solution)/shard_map/ppermute | solution.py:513
  22.6 12.3 %collective-permute-start.3 = (f32[2,256,256]{2,1,0:T(8,128)S(1)}, f32[2,256,256]{2,1,0:T(8,128)S(1)}, u32[]{:S(2)}, u32[]{:S(2)}) collective-permute-start(f32[2,256,256]{2,1,0:T(8,128)S(1)} %collective-permute-done.top_rim), channel_id=1, source_target_pairs={{16,0},{32,16},{48,32},{64,48},{80,64},{96,80},{112,96},{17,1},{33... | collective-permute-start | bytes 1572872 | tf_op jit(solution)/shard_map/ppermute | solution.py:513
  49.3 34.8 %collective-permute-start.11 = (f32[2,256,768]{2,1,0:T(8,128)S(1)}, f32[2,256,768]{2,1,0:T(8,128)S(1)}, u32[]{:S(2)}, u32[]{:S(2)}) collective-permute-start(f32[2,256,768]{2,1,0:T(8,128)S(1)} %get-tuple-element.34), channel_id=1, source_target_pairs={{0,16},{16,32},{32,48},{48,64},{64,80},{80,96},{96,112},{1,17},{17... | collective-permute-start | bytes 4718600 | tf_op jit(solution)/shard_map/ppermute | solution.py:513
  51.4 32.7 %collective-permute-start.12 = (f32[2,256,256]{2,1,0:T(8,128)S(1)}, f32[2,256,256]{2,1,0:T(8,128)S(1)}, u32[]{:S(2)}, u32[]{:S(2)}) collective-permute-start(f32[2,256,256]{2,1,0:T(8,128)S(1)} %get-tuple-element.35), channel_id=1, source_target_pairs={{0,1},{1,2},{2,3},{3,4},{4,5},{5,6},{6,7},{7,8},{8,9},{9,10},{10,1... | collective-permute-start | bytes 1572872 | tf_op jit(solution)/shard_map/ppermute | solution.py:513
  54.5 2.1 %collective-permute-start.4 = (f32[4,128,128]{2,1,0:T(8,128)S(1)}, f32[4,128,128]{2,1,0:T(8,128)S(1)}, u32[]{:S(2)}, u32[]{:S(2)}) collective-permute-start(f32[4,128,128]{2,1,0:T(8,128)S(1)} %get-tuple-element.28), channel_id=1, source_target_pairs={{0,16},{16,0},{32,48},{48,32},{64,80},{80,64},{96,112},{112,96},{1... | collective-permute-start | bytes 786440 | tf_op jit(solution)/shard_map/ppermute | solution.py:517
  56.6 10.3 %collective-permute-start.5 = (f32[128,128]{1,0:T(8,128)S(1)}, f32[128,128]{1,0:T(8,128)S(1)}, u32[]{:S(2)}, u32[]{:S(2)}) collective-permute-start(f32[128,128]{1,0:T(8,128)S(1)} %get-tuple-element.30), channel_id=1, source_target_pairs={{0,4},{1,5},{2,6},{3,7},{4,8},{5,9},{6,10},{7,11},{8,12},{9,13},{1... | collective-permute-start | bytes 196616 | tf_op jit(solution)/shard_map/ppermute | solution.py:525
  59.8 8.6 %collective-permute-start.6 = (f32[128,128]{1,0:T(8,128)S(1)}, f32[128,128]{1,0:T(8,128)S(1)}, u32[]{:S(2)}, u32[]{:S(2)}) collective-permute-start(f32[128,128]{1,0:T(8,128)S(1)} %get-tuple-element.31), channel_id=1, source_target_pairs={{0,8},{1,9},{2,10},{3,11},{4,12},{5,13},{6,14},{7,15},{8,0},{9,1},... | collective-permute-start | bytes 196616 | tf_op jit(solution)/shard_map/ppermute | solution.py:525
  65.0 3.5 %collective-permute-start.7 = (f32[128,128]{1,0:T(8,128)S(1)}, f32[128,128]{1,0:T(8,128)S(1)}, u32[]{:S(2)}, u32[]{:S(2)}) collective-permute-start(f32[128,128]{1,0:T(8,128)S(1)} %get-tuple-element.32), channel_id=1, source_target_pairs={{0,12},{1,13},{2,14},{3,15},{4,0},{5,1},{6,2},{7,3},{8,4},{9,5},{1... | collective-permute-start | bytes 196616 | tf_op jit(solution)/shard_map/ppermute | solution.py:525
  68.4 12.5 %collective-permute-start.10 = (f32[128,128]{1,0:T(8,128)S(1)}, f32[128,128]{1,0:T(8,128)S(1)}, u32[]{:S(2)}, u32[]{:S(2)}) collective-permute-start(f32[128,128]{1,0:T(8,128)S(1)} %y_sum.1.own), channel_id=1, source_target_pairs={{0,3},{1,0},{2,1},{3,2},{4,7},{5,4},{6,5},{7,6},{8,11},{9,8},{10,9... | collective-permute-start | bytes 196616 | tf_op jit(solution)/shard_map/ppermute | solution.py:529
  79.0 4.7 %collective-permute-start.9 = (f32[128,128]{1,0:T(8,128)S(1)}, f32[128,128]{1,0:T(8,128)S(1)}, u32[]{:S(2)}, u32[]{:S(2)}) collective-permute-start(f32[128,128]{1,0:T(8,128)S(1)} %y_sum.1.own), channel_id=1, source_target_pairs={{0,2},{1,3},{2,0},{3,1},{4,6},{5,7},{6,4},{7,5},{8,10},{9,11},{10,... | collective-permute-start | bytes 196616 | tf_op jit(solution)/shard_map/ppermute | solution.py:529
  79.0 5.0 %collective-permute-start.8 = (f32[128,128]{1,0:T(8,128)S(1)}, f32[128,128]{1,0:T(8,128)S(1)}, u32[]{:S(2)}, u32[]{:S(2)}) collective-permute-start(f32[128,128]{1,0:T(8,128)S(1)} %y_sum.1.own), channel_id=1, source_target_pairs={{0,1},{1,2},{2,3},{3,0},{4,5},{5,6},{6,7},{7,4},{8,9},{9,10},{10,1... | collective-permute-start | bytes 196616 | tf_op jit(solution)/shard_map/ppermute | solution.py:529
  84.2 13.8 %collective-permute-start.13 = (f32[2,256,256]{2,1,0:T(8,128)S(1)}, f32[2,256,256]{2,1,0:T(8,128)S(1)}, u32[]{:S(2)}, u32[]{:S(2)}) collective-permute-start(f32[2,256,256]{2,1,0:T(8,128)S(1)} %get-tuple-element.36), channel_id=1, source_target_pairs={{0,1},{1,2},{2,3},{3,4},{4,5},{5,6},{6,7},{7,8},{8,9},{9,10},{10,1... | collective-permute-start | bytes 1572872 | tf_op jit(solution)/shard_map/ppermute | solution.py:513
  85.5 4.8 %collective-permute-start.16 = (f32[128,128]{1,0:T(8,128)S(1)}, f32[128,128]{1,0:T(8,128)S(1)}, u32[]{:S(2)}, u32[]{:S(2)}) collective-permute-start(f32[128,128]{1,0:T(8,128)S(1)} %get-tuple-element.38.own), channel_id=1, source_target_pairs={{0,96},{16,112},{32,0},{48,16},{64,32},{80,48},{96,64},{112,80},{1... | collective-permute-start | bytes 196616 | tf_op jit(solution)/shard_map/ppermute | solution.py:521
  85.6 5.6 %collective-permute-start.15 = (f32[128,128]{1,0:T(8,128)S(1)}, f32[128,128]{1,0:T(8,128)S(1)}, u32[]{:S(2)}, u32[]{:S(2)}) collective-permute-start(f32[128,128]{1,0:T(8,128)S(1)} %get-tuple-element.38.own), channel_id=1, source_target_pairs={{0,64},{16,80},{32,96},{48,112},{64,0},{80,16},{96,32},{112,48},{1... | collective-permute-start | bytes 196616 | tf_op jit(solution)/shard_map/ppermute | solution.py:521
  89.5 5.2 %collective-permute-start.14 = (f32[128,128]{1,0:T(8,128)S(1)}, f32[128,128]{1,0:T(8,128)S(1)}, u32[]{:S(2)}, u32[]{:S(2)}) collective-permute-start(f32[128,128]{1,0:T(8,128)S(1)} %get-tuple-element.38.own), channel_id=1, source_target_pairs={{0,32},{16,48},{32,64},{48,80},{64,96},{80,112},{96,0},{112,16},{1... | collective-permute-start | bytes 196616 | tf_op jit(solution)/shard_map/ppermute | solution.py:521
  94.8 4.8 %collective-permute-start.19 = (f32[128,128]{1,0:T(8,128)S(1)}, f32[128,128]{1,0:T(8,128)S(1)}, u32[]{:S(2)}, u32[]{:S(2)}) collective-permute-start(f32[128,128]{1,0:T(8,128)S(1)} %x_sum.1.own), channel_id=1, source_target_pairs={{0,12},{1,13},{2,14},{3,15},{4,0},{5,1},{6,2},{7,3},{8,4},{9,5},{1... | collective-permute-start | bytes 196616 | tf_op jit(solution)/shard_map/ppermute | solution.py:525
  94.8 4.7 %collective-permute-start.18 = (f32[128,128]{1,0:T(8,128)S(1)}, f32[128,128]{1,0:T(8,128)S(1)}, u32[]{:S(2)}, u32[]{:S(2)}) collective-permute-start(f32[128,128]{1,0:T(8,128)S(1)} %x_sum.1.own), channel_id=1, source_target_pairs={{0,8},{1,9},{2,10},{3,11},{4,12},{5,13},{6,14},{7,15},{8,0},{9,1},... | collective-permute-start | bytes 196616 | tf_op jit(solution)/shard_map/ppermute | solution.py:525
  97.2 4.3 %collective-permute-start.17 = (f32[128,128]{1,0:T(8,128)S(1)}, f32[128,128]{1,0:T(8,128)S(1)}, u32[]{:S(2)}, u32[]{:S(2)}) collective-permute-start(f32[128,128]{1,0:T(8,128)S(1)} %x_sum.1.own), channel_id=1, source_target_pairs={{0,4},{1,5},{2,6},{3,7},{4,8},{5,9},{6,10},{7,11},{8,12},{9,13},{1... | collective-permute-start | bytes 196616 | tf_op jit(solution)/shard_map/ppermute | solution.py:525
  101.5 5.1 %collective-permute-start.20 = (f32[4,128,128]{2,1,0:T(8,128)S(1)}, f32[4,128,128]{2,1,0:T(8,128)S(1)}, u32[]{:S(2)}, u32[]{:S(2)}) collective-permute-start(f32[4,128,128]{2,1,0:T(8,128)S(1)} %half.1), channel_id=1, source_target_pairs={{0,16},{16,0},{32,48},{48,32},{64,80},{80,64},{96,112},{112,96},{1... | collective-permute-start | bytes 786440 | tf_op jit(solution)/shard_map/ppermute | solution.py:517
  (3 other events, 14.6 us)
